TPU v7x, 32 devices: a whole 2x2x4 slice. The times are simulated.
32 devices in a mesh: seq: 16 (over z, y, x), chan: 2 (over core).
Axes of the slice: x: 2, y: 2, z: 4, core: 2. Of those that a mesh axis runs over, the one named last changes fastest.
Arguments:
- gate_acts: bfloat16 [16384, 2048], P('seq', 'chan'), may hold values from -40 to 40
- value_acts: bfloat16 [16384, 2048], P('seq', 'chan'), may hold values from -6 to 6
- kernel: bfloat16 [32, 2048], P('chan'), may hold values from -0.125 to 0.125
- norm_gain: float32 [2048], P('chan'), may hold values from 0.1 to 1.9
- out_grad: bfloat16 [16384, 2048], P('seq', 'chan'), may hold values from -30 to 30
Outputs:
- normed: bfloat16 [16384, 2048], P('seq', 'chan')
- gate_grad: bfloat16 [16384, 2048], P('seq', 'chan')
- value_grad: bfloat16 [16384, 2048], P('seq', 'chan')
- kernel_grad: float32 [32, 2048], P('chan')
- gain_grad: float32 [2048], P('chan')
All inputs are finite; a program needn't handle non-finite values.
Results may differ from a plain program's by a relative error of at most 0.0085.
Values may be sent and summed in bfloat16 or wider, within the bound.
No kernel may reach another device: no remote copies, remote signals or barrier semaphores. Data moves between devices by JAX's collectives and lax.ppermute only.
A program may use at most 256 MiB of HBM per device.

v0:
```python
import math

import jax
import jax.numpy as jnp
from jax import lax
from jax.sharding import PartitionSpec as P

D = 2048


tile_cap = 256
norm_eps = 1e-06


def from_behind(value, axis, by):
    count = lax.axis_size(axis)
    pairs = [(i, i + by) for i in range(count) if 0 <= i + by < count]
    return lax.ppermute(value, axis, pairs)


def extended_2(block, sides, width):
    for axis, dim in sides:
        count = lax.axis_size(axis)
        forward = [(i, i + 1) for i in range(count - 1)]
        backward = [(target, source) for source, target in forward]
        low = lax.ppermute(
            lax.slice_in_dim(block, block.shape[dim] - width, None, axis=dim), axis, forward
        )
        high = lax.ppermute(lax.slice_in_dim(block, 0, width, axis=dim), axis, backward)
        block = jnp.concatenate([low, block, high], axis=dim)
    return block


def banded(row_vec, tile_rows, window_len):
    head_here = row_vec.shape[0]
    row_full = window_len + tile_rows
    wide_rows = jnp.broadcast_to(row_vec[:, None, :], (head_here, tile_rows, row_full))
    flat_rows = wide_rows.reshape(head_here, tile_rows * row_full)[:, : tile_rows * (row_full - 1)]
    return flat_rows.reshape(head_here, tile_rows, row_full - 1)[:, :, :window_len]


def windows(extended, tile_rows, out_count, slot_count):
    head_here, head_width, row_total = extended.shape
    tile_grid = extended.reshape(head_here, head_width, row_total // tile_rows, tile_rows)
    return jnp.concatenate(
        [
            tile_grid[:, :, slot_index : slot_index + out_count, :]
            for slot_index in range(slot_count)
        ],
        axis=3,
    )


def diagonal_sums(cross, lag_width):
    head_here, tile_rows, window_len = cross.shape
    flat_rows = cross.reshape(head_here, tile_rows * window_len)
    cut_at = (tile_rows - 1) * (window_len + 1)
    upper = flat_rows[:, :cut_at].reshape(head_here, tile_rows - 1, window_len + 1)[
        :, :, :lag_width
    ]
    return jnp.sum(upper, axis=1) + flat_rows[:, cut_at : cut_at + lag_width]


def on_device(gate_acts, value_acts, kernel, norm_gain, out_grad):
    row_count, chan_width = value_acts.shape
    head_here = kernel.shape[0]
    head_width = chan_width // head_here
    lag_span = kernel.shape[1] // 2
    tile_rows = min(tile_cap, lag_span)
    slot_count = 1 + 2 * lag_span // tile_rows
    window_len = tile_rows + 2 * lag_span
    local_count = row_count // tile_rows
    ahead_row = jnp.concatenate(
        [
            jnp.zeros((head_here, 1), kernel.dtype),
            kernel[:, ::-1],
            jnp.zeros((head_here, 2 * tile_rows - 1), kernel.dtype),
        ],
        axis=1,
    )
    behind_row = jnp.concatenate(
        [kernel, jnp.zeros((head_here, 2 * tile_rows), kernel.dtype)], axis=1
    )
    forward_band = banded(ahead_row, tile_rows, window_len)
    value_heads = value_acts.reshape(row_count, head_here, head_width).transpose(1, 2, 0)
    padded = jnp.pad(value_heads, ((0, 0), (0, 0), (2 * lag_span, 2 * lag_span)))
    spread_count = (row_count + 2 * lag_span) // tile_rows
    value_win = windows(padded, tile_rows, spread_count, slot_count)
    spread = jnp.einsum(
        "haw,hcpw->hcpa", forward_band, value_win, preferred_element_type=jnp.float32
    ).reshape(head_here, head_width, row_count + 2 * lag_span)
    from_below = from_behind(
        spread[:, :, row_count + lag_span :].astype(jnp.bfloat16), "seq", 1
    ).astype(jnp.float32)
    from_above = from_behind(spread[:, :, :lag_span].astype(jnp.bfloat16), "seq", -1).astype(
        jnp.float32
    )
    mixed_heads = spread[:, :, lag_span : lag_span + row_count] + from_below + from_above
    mixed_sum = mixed_heads.transpose(2, 0, 1).reshape(row_count, chan_width)
    hidden = gate_acts.astype(jnp.float32) * mixed_sum
    squares = jnp.sum(hidden * hidden, axis=1)
    weighted = norm_gain[None, :] * out_grad.astype(jnp.float32)
    squares = lax.psum(squares, "chan")
    scale = lax.rsqrt(squares / D + norm_eps)
    normed = (hidden * scale[:, None] * norm_gain[None, :]).astype(jnp.bfloat16)
    inner = lax.psum(jnp.sum(weighted * hidden, axis=1), "chan")
    hidden_grad = scale[:, None] * (weighted - hidden * (scale * scale * inner / D)[:, None])
    gate_grad = (hidden_grad * mixed_sum).astype(jnp.bfloat16)
    mix_grad = (hidden_grad * gate_acts.astype(jnp.float32)).astype(jnp.bfloat16)
    gain_local = jnp.sum(out_grad.astype(jnp.float32) * hidden * scale[:, None], axis=0)
    mix_heads = mix_grad.reshape(row_count, head_here, head_width).transpose(1, 2, 0)
    grad_outer = extended_2(mix_heads, (("seq", 2),), lag_span)
    grad_win = windows(grad_outer, tile_rows, local_count, slot_count)
    backward_band = banded(behind_row, tile_rows, window_len)
    value_sum = jnp.einsum(
        "haw,hcpw->hcpa", backward_band, grad_win, preferred_element_type=jnp.float32
    )
    value_grad = (
        value_sum.reshape(head_here, head_width, row_count)
        .transpose(2, 0, 1)
        .reshape(row_count, chan_width)
        .astype(jnp.bfloat16)
    )
    value_tiles = value_heads.reshape(head_here, head_width, local_count, tile_rows)
    cross = jnp.einsum("hcpa,hcpw->haw", value_tiles, grad_win, preferred_element_type=jnp.float32)
    kernel_local = diagonal_sums(cross, 2 * lag_span)
    kernel_total, gain_total = lax.psum((kernel_local, gain_local), "seq")
    tokens = row_count * lax.axis_size("seq")
    kernel_grad = kernel_total / math.sqrt(tokens * head_width)
    gain_grad = gain_total / math.sqrt(tokens)
    return (normed, gate_grad, value_grad, kernel_grad, gain_grad)


def solution(mesh):
    placed = (P("seq", "chan"), P("seq", "chan"), P("chan", None), P("chan"), P("seq", "chan"))
    return jax.shard_map(
        on_device,
        mesh=mesh,
        in_specs=placed,
        out_specs=(
            P("seq", "chan"),
            P("seq", "chan"),
            P("seq", "chan"),
            P("chan", None),
            P("chan"),
        ),
        check_vma=False,
    )
```

profile of v0, /device:TPU:0, one launch (start us, length us, event | category | flops | bytes accessed | tf_op | source)
XLA Modules:
  0.0 966.6 jit_solution(6224744742704965668)
XLA Ops:
  15.3 18.3 %reshape.59 = bf16[16,64,20,256]{3,2,1,0:T(8,128)(2,1)} reshape(bf16[16,64,5120]{2,1,0:T(8,128)(2,1)} %pad.5) | data formatting | bytes 20971520 | tf_op jit(solution)/shard_map/reshape | solution.py:44
  33.6 65.2 %fusion.14 = (bf16[16,64,12,256]{3,2,1,0:T(8,128)(2,1)}, bf16[16,64,12,256]{3,2,1,0:T(8,128)(2,1)}, bf16[16,64,12,256]{3,2,1,0:T(8,128)(2,1)}, bf16[16,64,12,256...) fusion(bf16[16,64,20,256]{3,2,1,0:T(8,128)(2,1)} %reshape.59), kind=kLoop, calls=%fused_computation.51 | loop fusion | bytes 113246208 | tf_op jit(solution)/shard_map/slice | solution.py:47
  107.7 50.3 %copy.62 = bf16[2,8,256,2560]{3,1,2,0:T(8,128)(2,1)S(1)} copy(bf16[2,8,256,2560]{3,2,1,0:T(8,128)(2,1)S(1)} %bitcast.70) | data formatting | bytes 41943040
  166.0 65.4 %reshape.61 = bf16[16,256,2559]{2,1,0:T(8,128)(2,1)} reshape(bf16[16,655104]{1,0:T(8,128)(2,1)} %slice.123) | data formatting | bytes 41926656 | tf_op jit(solution)/shard_map/reshape | solution.py:39
  231.5 9.2 copy_dynamic-update-slice_fusion.7
  240.7 9.1 copy_dynamic-update-slice_fusion.6
  255.3 9.1 copy_dynamic-update-slice_fusion.4
  264.4 9.2 copy_dynamic-update-slice_fusion.3
  279.0 9.1 copy_dynamic-update-slice_fusion.1
  293.7 31.6 %fusion.4 = f32[16,12,8,8,256]{4,3,2,1,0:T(8,128)} fusion(bf16[16,64,12,2304]{3,1,2,0:T(8,128)(2,1)} %copy_dynamic-update-slice_fusion, bf16[16,256,2559]{2,1,0:T(8,128)(2,1)} %reshape.61), kind=kOutput, calls=%fused_computation.22 | convolution fusion | flops 14495514624 | bytes 88080384 | tf_op jit(solution)/shard_map/haw,hcpw->hcpa/dot_general | solution.py:89
  325.3 11.1 %copy.60 = f32[16,12,8,8,256]{4,3,1,2,0:T(8,128)} copy(f32[16,12,8,8,256]{4,3,2,1,0:T(8,128)} %fusion.4) | data formatting | bytes 25165824 | tf_op jit(solution)/shard_map/reshape | solution.py:91
  358.7 80.7 %collective-permute-done = bf16[16,64,1024]{2,1,0:T(8,128)(2,1)} collective-permute-done((bf16[16,64,1024]{2,1,0:T(8,128)(2,1)}, bf16[16,64,1024]{2,1,0:T(8,128)(2,1)}, u32[]{:S(2)}, u32[]{:S(2)}) %collective-permute-start) | collective-permute-done | bytes 2097184 | tf_op jit(solution)/shard_map/ppermute | solution.py:18
  473.5 50.3 %copy.63 = bf16[2,8,256,2560]{3,1,2,0:T(8,128)(2,1)S(1)} copy(bf16[2,8,256,2560]{3,2,1,0:T(8,128)(2,1)S(1)} %bitcast.71) | data formatting | bytes 41943040
  531.8 64.9 %reshape.67 = bf16[16,256,2559]{2,1,0:T(8,128)(2,1)} reshape(bf16[16,655104]{1,0:T(8,128)(2,1)} %slice.137) | data formatting | bytes 41926656 | tf_op jit(solution)/shard_map/reshape | solution.py:39
  603.2 41.6 %psum.31 = f32[1024]{0:T(1024)S(1)} all-reduce(f32[1024]{0:T(1024)S(1)} %get-tuple-element.10), channel_id=1, replica_groups=mesh['seq'=16,'chan'=2] {'seq'}, use_global_device_ids=true, to_apply=%region_7.8 | all-reduce | flops 1024 | bytes 8192 | tf_op jit(solution)/shard_map/psum | solution.py:127
  651.6 12.0 %reshape.65 = bf16[16,64,12,256]{3,2,1,0:T(8,128)(2,1)} reshape(bf16[16,64,3072]{2,1,0:T(8,128)(2,1)} %pad_maximum_fusion) | data formatting | bytes 12582912 | tf_op jit(solution)/shard_map/reshape | solution.py:44
  663.7 22.0 %fusion.15 = (bf16[16,64,4,256]{3,2,1,0:T(4,128)(2,1)S(1)}, bf16[16,64,4,256]{3,2,1,0:T(4,128)(2,1)S(1)}, bf16[16,64,4,256]{3,2,1,0:T(4,128)(2,1)S(1)}, bf16[16,...) fusion(bf16[16,64,12,256]{3,2,1,0:T(8,128)(2,1)} %reshape.65), kind=kLoop, calls=%fused_computation.52 | loop fusion | bytes 37748736 | tf_op jit(solution)/shard_map/slice | solution.py:47
  695.8 19.0 %convolution_bitcast_fusion = f32[16,256,2304]{1,2,0:T(8,128)} fusion(bf16[16,64,4,2304]{3,1,2,0:T(8,128)(2,1)} %copy-done.5, bf16[16,8,4,8,256]{4,3,2,1,0:T(8,128)(2,1)S(1)} %bitcast.84), kind=kOutput, calls=%fused_computation.1 | convolution fusion | flops 4831838208 | bytes 58720256 | tf_op jit(solution)/shard_map/hcpa,hcpw->haw/dot_general | solution.py:125
  714.8 37.8 %copy.64 = f32[2,8,256,2304]{3,1,2,0:T(8,128)} copy(f32[2,8,256,2304]{2,3,1,0:T(8,128)} %bitcast.76) | data formatting | bytes 75497472
  752.6 27.0 %slice.139 = f32[16,587775]{1,0:T(8,128)} slice(f32[16,589824]{1,0:T(8,128)} %bitcast.68), slice={[0:16], [0:587775]} | slice | bytes 75235200 | tf_op jit(solution)/shard_map/slice | solution.py:58
  779.6 64.7 %reshape.70 = f32[16,255,2305]{2,1,0:T(8,128)} reshape(f32[16,587775]{1,0:T(8,128)} %slice.139) | data formatting | bytes 75235200 | tf_op jit(solution)/shard_map/reshape | solution.py:58
  844.4 11.6 %slice_reduce_fusion = f32[16,2048]{1,0:T(8,128)S(1)} fusion(f32[16,255,2305]{2,1,0:T(8,128)} %reshape.70), kind=kLoop, calls=%fused_computation | loop fusion | flops 8323072 | bytes 33554432 | tf_op jit(solution)/shard_map/reduce_sum | solution.py:61
  857.7 14.3 %convert_bitcast_fusion = bf16[16,4,8,8,256]{4,3,2,1,0:T(8,128)(2,1)S(1)} fusion(bf16[16,64,4,2304]{3,1,2,0:T(8,128)(2,1)} %copy-done.5, bf16[16,256,2559]{2,1,0:T(8,128)(2,1)} %reshape.67), kind=kOutput, calls=%fused_computation.45 | convolution fusion | flops 4832886784 | bytes 39845888 | tf_op jit(solution)/shard_map/haw,hcpw->hcpa/dot_general | solution.py:115
  874.8 83.1 %all-reduce.4.cloned.1.call-done = f32[16,2048]{1,0:T(8,128)} async-done(((f32[16,2048]{1,0:T(8,128)}), f32[16,2048]{1,0:T(8,128)}) %all-reduce.4.cloned.1.call-update) | async-done | bytes 131088 | tf_op jit(solution)/shard_map/psum | solution.py:127
  (82 shorter events, 135.1 us)
Async XLA Ops:
  7.2 950.8 %all-reduce.4.cloned.1.call-start = ((), (), s32[]{:S(2)}) async-start(), calls=%async_computation | async-start | bytes 262144 | tf_op jit(solution)/shard_map/psum | solution.py:127
  10.1 5.2 copy-start.1
  98.9 5.7 copy-start.4
  231.5 18.4 %slice-start.4 = ((s8[8388608]{0:T(1024)(128)(4,1)}), s8[4194304]{0:T(1024)(128)(4,1)S(1)}, s32[]{:S(2)}) async-start(s8[8388608]{0:T(1024)(128)(4,1)} %bitcast.81), calls=%async_computation.5 | async-start | bytes 8388608
  240.7 9.1 slice-start.5
  255.3 18.3 %slice-start.2 = ((s8[8388608]{0:T(1024)(128)(4,1)}), s8[4194304]{0:T(1024)(128)(4,1)S(1)}, s32[]{:S(2)}) async-start(s8[8388608]{0:T(1024)(128)(4,1)} %bitcast.79), calls=%async_computation.3 | async-start | bytes 8388608
  264.4 9.2 slice-start.3
  273.6 14.5 %slice-start = ((s8[8388608]{0:T(1024)(128)(4,1)}), s8[4194304]{0:T(1024)(128)(4,1)S(1)}, s32[]{:S(2)}) async-start(s8[8388608]{0:T(1024)(128)(4,1)} %bitcast.77), calls=%async_computation.1 | async-start | bytes 8388608
  279.0 9.1 slice-start.1
  344.4 95.0 %collective-permute-start = (bf16[16,64,1024]{2,1,0:T(8,128)(2,1)}, bf16[16,64,1024]{2,1,0:T(8,128)(2,1)}, u32[]{:S(2)}, u32[]{:S(2)}) collective-permute-start(bf16[16,64,1024]{2,1,0:T(8,128)(2,1)} %get-tuple-element.33), channel_id=1, source_target_pairs={{0,2},{2,4},{4,6},{6,8},{8,10},{10,12},{12,14},{14,16},{16,18},{18... | collective-permute-start | bytes 6291464 | tf_op jit(solution)/shard_map/ppermute | solution.py:18
  350.6 90.7 %collective-permute-start.1 = (bf16[16,64,1024]{2,1,0:T(8,128)(2,1)}, bf16[16,64,1024]{2,1,0:T(8,128)(2,1)}, u32[]{:S(2)}, u32[]{:S(2)}) collective-permute-start(bf16[16,64,1024]{2,1,0:T(8,128)(2,1)} %get-tuple-element.34), channel_id=1, source_target_pairs={{2,0},{4,2},{6,4},{8,6},{10,8},{12,10},{14,12},{16,14},{18,16},{20... | collective-permute-start | bytes 6291464 | tf_op jit(solution)/shard_map/ppermute | solution.py:18
  358.7 92.4 %copy-start.6 = (f32[1024]{0:T(1024)S(1)}, f32[1024]{0:T(1024)}, u32[]{:S(2)}) copy-start(f32[1024]{0:T(1024)} %param.8) | copy-start | bytes 12292
  445.8 2.0 copy-start
  465.2 180.1 %collective-permute-start.2 = (bf16[16,64,1024]{2,1,0:T(8,128)(2,1)}, bf16[16,64,1024]{2,1,0:T(8,128)(2,1)}, u32[]{:S(2)}, u32[]{:S(2)}) collective-permute-start(bf16[16,64,1024]{2,1,0:T(8,128)(2,1)} %bitcast.8), channel_id=1, source_target_pairs={{0,2},{2,4},{4,6},{6,8},{8,10},{10,12},{12,14},{14,16},{16,18},{18... | collective-permute-start | bytes 6291464 | tf_op jit(solution)/shard_map/ppermute | solution.py:26
  470.0 175.4 %collective-permute-start.3 = (bf16[16,64,1024]{2,1,0:T(8,128)(2,1)}, bf16[16,64,1024]{2,1,0:T(8,128)(2,1)}, u32[]{:S(2)}, u32[]{:S(2)}) collective-permute-start(bf16[16,64,1024]{2,1,0:T(8,128)(2,1)} %bitcast.8), channel_id=1, source_target_pairs={{2,0},{4,2},{6,4},{8,6},{10,8},{12,10},{14,12},{16,14},{18,16},{20... | collective-permute-start | bytes 6291464 | tf_op jit(solution)/shard_map/ppermute | solution.py:29
  531.8 68.9 %copy-start.3 = (bf16[1024,1024]{0,1:T(8,128)(2,1)S(1)}, bf16[1024,1024]{0,1:T(8,128)(2,1)}, u32[]{:S(2)}) copy-start(bf16[1024,1024]{0,1:T(8,128)(2,1)} %get-tuple-element.22) | copy-start | bytes 6291460
  687.7 8.1 copy-start.2
  689.4 6.3 copy-start.5
Sparse Core Ops, SparseCore 0:
  857.8 100.0 all-reduce.3
where the time goes:
time: 976 us; the launch traced here: 967 us
  local copies, waits for them, and re-layouts  617 us (63%)
  waiting for transfers between devices  166 us (17%)
  matrix products  64.9 us (7%)
  blocking collectives  46.5 us (5%)
  other arithmetic  44.2 us (5%)
  between operations  14.6 us (1%)
  starting transfers between devices  13.5 us (1%)
    unnamed x51, local copies, waits for them, and re-layouts  231 us
    reshape x2, local copies, waits for them, and re-layouts, banded(): flat_rows.reshape(head_here, tile_rows, row_full - 1)[:, :, :window_len]  130 us
    slice x2, local copies, waits for them, and re-layouts, windows(): tile_grid[:, :, slot_index:slot_index + out_count, :]  87.2 us
    psum x1, waiting for transfers between devices, on_device(): kernel_total, gain_total = lax.psum((kernel_local, gain_local), 'seq')  83.1 us
    ppermute x2, waiting for transfers between devices, from_behind(): return lax.ppermute(value, axis, pairs)  82.6 us
    reshape x1, local copies, waits for them, and re-layouts, diagonal_sums(): flat_rows[:, :cut_at].reshape(head_here, tile_rows - 1, window_len + 1)  64.7 us
    psum x1, blocking collectives, on_device(): kernel_total, gain_total = lax.psum((kernel_local, gain_local), 'seq')  41.6 us
    dot_general x1, matrix products, on_device(): jnp.einsum('haw,hcpw->hcpa', forward_band, value_win, preferred_element_t...  31.6 us
  transfers between devices with their start and end apart: 5, of which 3 were waited for; matrix products, arithmetic and copies ran while one was open for 16% of the time, Pallas kernels for 0%

commit v1 on v0

v1 whole, which is shorter than its diff:
```python
import functools
import math

import jax
import jax.numpy as jnp
from jax import lax
from jax.experimental import pallas as pl
from jax.experimental.pallas import tpu as pltpu
from jax.sharding import PartitionSpec as P

norm_eps = 1e-06
TILE = 256
LANES = 128
HEAD = 64
CHUNKS = 4
MIB = 1 << 20


def params(mib, rank=1):
    return pltpu.CompilerParams(
        vmem_limit_bytes=mib * MIB, dimension_semantics=("arbitrary",) * rank
    )


def lane_iota(rows):
    return lax.broadcasted_iota(jnp.int32, (rows, LANES), 1)


def band_body(row_ref, band_ref):
    tiles = row_ref.shape[2] // LANES
    upper = lane_iota(LANES) >= lax.broadcasted_iota(jnp.int32, (LANES, LANES), 0)
    for head in range(row_ref.shape[1]):
        before = jnp.zeros((LANES, LANES), jnp.float32)
        band_ref[head, :, :LANES] = before.astype(band_ref.dtype)
        for tile in range(tiles):
            segment = row_ref[0, head : head + 1, tile * LANES : (tile + 1) * LANES]
            turned = pltpu.roll(
                jnp.broadcast_to(segment, (LANES, LANES)), 0, 1, stride=1, stride_axis=0
            )
            cell = jnp.where(upper, turned, before)
            band_ref[head, :, (tile + 1) * LANES : (tile + 2) * LANES] = cell.astype(
                band_ref.dtype
            )
            before = turned


def bands(rows):
    heads, length = rows.shape
    return pl.pallas_call(
        band_body,
        grid=(heads // 2,),
        in_specs=[pl.BlockSpec((1, 2, length), lambda g: (g, 0, 0))],
        out_specs=pl.BlockSpec((2, LANES, length + LANES), lambda g: (g, 0, 0)),
        out_shape=jax.ShapeDtypeStruct((heads, LANES, length + LANES), jnp.bfloat16),
        compiler_params=params(16),
        name="bands",
    )(rows.reshape(heads // 2, 2, length))


def lay_out(slabs, even_ref, odd_ref):
    low = lane_iota(TILE) < HEAD
    turned = [pltpu.roll(slab, HEAD, 1) for slab in slabs]
    for tile in range(len(slabs) // 2):
        cols = slice(tile * LANES, (tile + 1) * LANES)
        first, second = 2 * tile, 2 * tile + 1
        even_ref[0, :, cols] = jnp.where(low, slabs[first], turned[second])
        even_ref[1, :, cols] = jnp.where(low, turned[first], slabs[second])
        if odd_ref is not None and second + 1 < len(slabs):
            odd_ref[0, :, cols] = jnp.where(low, slabs[second], turned[second + 1])
            odd_ref[1, :, cols] = jnp.where(low, turned[second], slabs[second + 1])


def window(even_ref, odd_ref, head, start, width):
    if start % 2 == 0:
        return even_ref[head, :, start * HEAD : start * HEAD + width]
    return odd_ref[head, :, (start - 1) * HEAD : (start - 1) * HEAD + width]


def gather_slabs(odd_dev, own_ref, near_refs, far_refs):
    def pieces(refs):
        return [
            ref[row : row + TILE, :] for ref in refs for row in range(0, ref.shape[0], TILE)
        ]

    near, far, own = pieces(near_refs), pieces(far_refs), pieces([own_ref])
    left = [jnp.where(odd_dev, n, f) for n, f in zip(near, far)]
    right = [jnp.where(odd_dev, f, n) for n, f in zip(near, far)]
    return left + own + right


def band_product(band_ref, even_ref, odd_ref, head, slots, width):
    total = None
    for slot in range(slots):
        at = slot * TILE
        tile = jnp.concatenate(
            [
                band_ref[head, :, LANES + at : LANES + at + TILE],
                band_ref[head, :, at : at + TILE],
            ],
            axis=0,
        )
        part = jnp.dot(
            tile,
            window(even_ref, odd_ref, head, slot, width),
            preferred_element_type=jnp.float32,
        )
        total = part if total is None else total + part
    return total


def token_blocks(first, second):
    low = lane_iota(TILE) < HEAD
    blocks = []
    for tile in range(first.shape[1] // LANES):
        cols = slice(tile * LANES, (tile + 1) * LANES)
        one, two = first[:, cols], second[:, cols]
        blocks.append(jnp.where(low, one, pltpu.roll(two, HEAD, 1)))
        blocks.append(jnp.where(low, pltpu.roll(one, HEAD, 1), two))
    return blocks


def forward_body(slots, odd_ref_scalar, band_ref, own_ref, *refs):
    near_refs, far_refs = refs[:CHUNKS], refs[CHUNKS : 2 * CHUNKS]
    gate_ref, grad_ref, gain_ref, mixed_ref, sums_ref = refs[2 * CHUNKS : 2 * CHUNKS + 5]
    even_ref, odd_ref, square_ref, inner_ref = refs[2 * CHUNKS + 5 :]
    step = pl.program_id(0)

    @pl.when(step == 0)
    def _():
        square_ref[...] = jnp.zeros_like(square_ref)
        inner_ref[...] = jnp.zeros_like(inner_ref)

    rows = own_ref.shape[0]
    width = rows // TILE * HEAD
    lay_out(
        gather_slabs(odd_ref_scalar[0] == 1, own_ref, near_refs, far_refs), even_ref, odd_ref
    )
    results = [
        band_product(band_ref, even_ref, odd_ref, head, slots, width) for head in range(2)
    ]
    for index, mixed in enumerate(token_blocks(*results)):
        at = slice(index * TILE, (index + 1) * TILE)
        mixed_ref[at, :] = mixed
        hidden = gate_ref[at, :].astype(jnp.float32) * mixed
        weighted = gain_ref[...] * grad_ref[at, :].astype(jnp.float32)
        square_ref[at, :] += hidden * hidden
        inner_ref[at, :] += weighted * hidden

    @pl.when(step == pl.num_programs(0) - 1)
    def _():
        for at in range(0, rows, LANES):
            cols = slice(at, at + LANES)
            sums_ref[0:1, cols] = jnp.sum(square_ref[cols, :].T, axis=0, keepdims=True)
            sums_ref[1:2, cols] = jnp.sum(inner_ref[cols, :].T, axis=0, keepdims=True)


def slab_spec(rows):
    return pl.BlockSpec((rows, LANES), lambda g: (0, g))


def band_spec(band):
    return pl.BlockSpec((2,) + band.shape[1:], lambda g: (g, 0, 0))


def chunk_specs(chunks):
    return [slab_spec(chunk.shape[0]) for chunk in chunks]


SCALAR = pl.BlockSpec(memory_space=pltpu.SMEM)


def layout_scratch(rows, lag):
    blocks = (rows + 2 * lag) // TILE
    return [
        pltpu.VMEM((2, TILE, blocks * HEAD), jnp.bfloat16),
        pltpu.VMEM((2, TILE, blocks * HEAD - LANES), jnp.bfloat16),
    ]


def forward(odd_dev, band, own, near, far, gate, grad, gain, lag):
    rows, width = own.shape
    slots = 1 + 2 * lag // TILE
    flops = 2 * (width // HEAD) * TILE * TILE * slots * rows // TILE * HEAD
    return pl.pallas_call(
        functools.partial(forward_body, slots),
        grid=(width // LANES,),
        in_specs=[SCALAR, band_spec(band), slab_spec(rows)]
        + chunk_specs(near)
        + chunk_specs(far)
        + [slab_spec(rows), slab_spec(rows), slab_spec(1)],
        out_specs=[slab_spec(rows), pl.BlockSpec((2, rows), lambda g: (0, 0))],
        out_shape=[
            jax.ShapeDtypeStruct((rows, width), jnp.float32),
            jax.ShapeDtypeStruct((2, rows), jnp.float32),
        ],
        scratch_shapes=layout_scratch(rows, lag)
        + [pltpu.VMEM((rows, LANES), jnp.float32)] * 2,
        compiler_params=params(32),
        cost_estimate=pl.CostEstimate(
            flops=flops, bytes_accessed=16 * rows * width, transcendentals=0
        ),
        name="forward",
    )(odd_dev, band, own, *near, *far, gate, grad, gain)


def token_columns(full_width, sums_ref, scale_ref, pull_ref):
    for at in range(0, sums_ref.shape[1], LANES):
        cols = slice(at, at + LANES)
        scale = lax.rsqrt(sums_ref[0:1, cols] / full_width + norm_eps)
        pull = scale * scale * sums_ref[1:2, cols] / full_width
        scale_ref[cols, :] = jnp.broadcast_to(scale, (LANES, LANES)).T
        pull_ref[cols, :] = jnp.broadcast_to(pull, (LANES, LANES)).T


def mix_grad_body(full_width, sums_ref, mixed_ref, gate_ref, grad_ref, gain_ref, out_ref, *scratch):
    scale_ref, pull_ref = scratch

    @pl.when(pl.program_id(0) == 0)
    def _():
        token_columns(full_width, sums_ref, scale_ref, pull_ref)

    for at in range(0, mixed_ref.shape[0], LANES):
        rows = slice(at, at + LANES)
        gate = gate_ref[rows, :].astype(jnp.float32)
        hidden = gate * mixed_ref[rows, :]
        weighted = gain_ref[...] * grad_ref[rows, :].astype(jnp.float32)
        hidden_grad = scale_ref[rows, :] * (weighted - hidden * pull_ref[rows, :])
        out_ref[rows, :] = (hidden_grad * gate).astype(out_ref.dtype)


def norm_body(full_width, sums_ref, mixed_ref, gate_ref, grad_ref, gain_ref, *refs):
    normed_ref, gate_grad_ref, gain_grad_ref, scale_ref, pull_ref = refs

    @pl.when(pl.program_id(0) == 0)
    def _():
        token_columns(full_width, sums_ref, scale_ref, pull_ref)

    gain = gain_ref[...]
    total = jnp.zeros((8, LANES), jnp.float32)
    for at in range(0, mixed_ref.shape[0], LANES):
        rows = slice(at, at + LANES)
        gate = gate_ref[rows, :].astype(jnp.float32)
        mixed = mixed_ref[rows, :]
        grad = grad_ref[rows, :].astype(jnp.float32)
        scale = scale_ref[rows, :]
        hidden = gate * mixed
        scaled = hidden * scale
        normed_ref[rows, :] = (scaled * gain).astype(normed_ref.dtype)
        hidden_grad = scale * (gain * grad - hidden * pull_ref[rows, :])
        gate_grad_ref[rows, :] = (hidden_grad * mixed).astype(gate_grad_ref.dtype)
        total += jnp.sum((grad * scaled).reshape(LANES // 8, 8, LANES), axis=0)
    gain_grad_ref[...] = jnp.sum(total, axis=0, keepdims=True)


def norm_call(body, out_shape, name, full_width, sums, mixed, gate, grad, gain):
    rows, width = mixed.shape
    return pl.pallas_call(
        functools.partial(body, full_width),
        grid=(width // LANES,),
        in_specs=[pl.BlockSpec((2, rows), lambda g: (0, 0))]
        + [slab_spec(rows)] * 3
        + [slab_spec(1)],
        out_specs=jax.tree.map(lambda s: slab_spec(s.shape[0]), out_shape),
        out_shape=out_shape,
        scratch_shapes=[pltpu.VMEM((rows, LANES), jnp.float32)] * 2,
        compiler_params=params(24),
        cost_estimate=pl.CostEstimate(
            flops=10 * rows * width, bytes_accessed=12 * rows * width, transcendentals=0
        ),
        name=name,
    )(sums, mixed, gate, grad, gain)


def kernel_grad_body(slots, odd_ref_scalar, mix_ref, own_ref, *refs):
    near_refs, far_refs = refs[:CHUNKS], refs[CHUNKS : 2 * CHUNKS]
    out_ref, even_ref, odd_ref, mix_even_ref, cells_ref = refs[2 * CHUNKS :]
    rows = own_ref.shape[0]
    width = rows // TILE * HEAD
    lay_out(
        gather_slabs(odd_ref_scalar[0] == 1, own_ref, near_refs, far_refs), even_ref, odd_ref
    )
    lay_out([mix_ref[at : at + TILE, :] for at in range(0, rows, TILE)], mix_even_ref, None)
    span = cells_ref.shape[1]
    for head in range(2):
        mix = mix_even_ref[head]
        carry = None
        for lag_slot in range(slots):
            cross = lax.dot_general(
                window(even_ref, odd_ref, head, slots - 1 - lag_slot, width),
                mix,
                (((1,), (1,)), ((), ())),
                preferred_element_type=jnp.float32,
            )
            at = 2 * lag_slot * LANES
            upper, lower = cross[:LANES], cross[LANES:]
            if carry is not None:
                cells_ref[:, at - LANES : at] = carry + lower[:, :LANES]
            cells_ref[:, at : at + LANES] = upper[:, :LANES] + lower[:, LANES:]
            carry = upper[:, LANES:]
        total = cells_ref[0:8, :]
        for group in range(1, LANES // 8):
            total += pltpu.roll(cells_ref[8 * group : 8 * group + 8, :], span - 8 * group, 1)
        row = lax.broadcasted_iota(jnp.int32, (8, span), 0)
        for bit in (1, 2, 4):
            total = jnp.where((row & bit) != 0, pltpu.roll(total, span - bit, 1), total)
        out_ref[0, head : head + 1, :] = jnp.sum(total, axis=0, keepdims=True)[
            :, : out_ref.shape[2]
        ]


def kernel_grad_local(odd_dev, mix_grad, own, near, far, lag):
    rows, width = own.shape
    slots = 1 + 2 * lag // TILE
    pairs = width // LANES
    flops = 2 * (width // HEAD) * TILE * TILE * slots * rows // TILE * HEAD
    out = pl.pallas_call(
        functools.partial(kernel_grad_body, slots),
        grid=(pairs,),
        in_specs=[SCALAR, slab_spec(rows), slab_spec(rows)]
        + chunk_specs(near)
        + chunk_specs(far),
        out_specs=pl.BlockSpec((1, 2, 2 * lag), lambda g: (g, 0, 0)),
        out_shape=jax.ShapeDtypeStruct((pairs, 2, 2 * lag), jnp.float32),
        scratch_shapes=layout_scratch(rows, lag)
        + [
            pltpu.VMEM((2, TILE, rows // TILE * HEAD), jnp.bfloat16),
            pltpu.VMEM((LANES, 2 * lag + LANES), jnp.float32),
        ],
        compiler_params=params(32),
        cost_estimate=pl.CostEstimate(
            flops=flops, bytes_accessed=8 * rows * width, transcendentals=0
        ),
        name="kernel_grad",
    )(odd_dev, mix_grad, own, *near, *far)
    return out.reshape(2 * pairs, 2 * lag)


def value_grad_body(slots, odd_ref_scalar, band_ref, own_ref, *refs):
    near_refs, far_refs = refs[:CHUNKS], refs[CHUNKS : 2 * CHUNKS]
    out_ref, even_ref, odd_ref = refs[2 * CHUNKS :]
    width = own_ref.shape[0] // TILE * HEAD
    lay_out(
        gather_slabs(odd_ref_scalar[0] == 1, own_ref, near_refs, far_refs), even_ref, odd_ref
    )
    results = [
        band_product(band_ref, even_ref, odd_ref, head, slots, width) for head in range(2)
    ]
    for index, block in enumerate(token_blocks(*results)):
        out_ref[index * TILE : (index + 1) * TILE, :] = block.astype(out_ref.dtype)


def value_grad_of(odd_dev, band, own, near, far, lag):
    rows, width = own.shape
    slots = 1 + 2 * lag // TILE
    flops = 2 * (width // HEAD) * TILE * TILE * slots * rows // TILE * HEAD
    return pl.pallas_call(
        functools.partial(value_grad_body, slots),
        grid=(width // LANES,),
        in_specs=[SCALAR, band_spec(band), slab_spec(rows)]
        + chunk_specs(near)
        + chunk_specs(far),
        out_specs=slab_spec(rows),
        out_shape=jax.ShapeDtypeStruct((rows, width), jnp.bfloat16),
        scratch_shapes=layout_scratch(rows, lag),
        compiler_params=params(32),
        cost_estimate=pl.CostEstimate(
            flops=flops, bytes_accessed=12 * rows * width, transcendentals=0
        ),
        name="value_grad",
    )(odd_dev, band, own, *near, *far)


def neighbours(block):
    count = lax.axis_size("seq")
    swap = [(i, i ^ 1) for i in range(count)]
    relay = [(i, i + 2) if i % 2 == 0 else (i, i - 2) for i in range(count)]
    relay = [(source, target) for source, target in relay if 0 <= target < count]
    size = block.shape[0] // CHUNKS
    near = [
        lax.ppermute(block[c * size : (c + 1) * size], "seq", swap) for c in range(CHUNKS)
    ]
    far = [lax.ppermute(piece, "seq", relay) for piece in near]
    return near, far


def sum_over_seq(value):
    count = lax.axis_size("seq")
    if count & (count - 1):
        return lax.psum(value, "seq")
    step = 1
    while step < count:
        value = value + lax.ppermute(value, "seq", [(i, i ^ step) for i in range(count)])
        step *= 2
    return value


def on_device(gate_acts, value_acts, kernel, norm_gain, out_grad):
    rows, width = value_acts.shape
    heads = kernel.shape[0]
    lag = kernel.shape[1] // 2
    assert width == heads * HEAD and rows == lag and rows % TILE == 0
    full_width = width * lax.axis_size("chan")
    odd_dev = (lax.axis_index("seq") % 2).astype(jnp.int32).reshape(1)
    gain = norm_gain.reshape(1, width)

    near, far = neighbours(value_acts)
    taps = kernel.astype(jnp.float32)
    band = bands(jnp.pad(taps[:, ::-1], ((0, 0), (1, TILE - 1))))
    mixed, sums = forward(
        odd_dev, band, value_acts, near, far, gate_acts, out_grad, gain, lag
    )
    sums = lax.psum(sums, "chan")
    big = jax.ShapeDtypeStruct((rows, width), jnp.bfloat16)
    args = (full_width, sums, mixed, gate_acts, out_grad, gain)
    mix_grad = norm_call(mix_grad_body, big, "mix_grad", *args)
    grad_near, grad_far = neighbours(mix_grad)
    normed, gate_grad, gain_local = norm_call(
        norm_body, [big, big, jax.ShapeDtypeStruct((1, width), jnp.float32)], "norm", *args
    )
    kernel_local = kernel_grad_local(odd_dev, mix_grad, value_acts, near, far, lag)
    totals = sum_over_seq(
        jnp.concatenate([kernel_local, gain_local.reshape(heads, HEAD)], axis=1)
    )
    back_band = bands(jnp.pad(taps, ((0, 0), (0, TILE))))
    value_grad = value_grad_of(odd_dev, back_band, mix_grad, grad_near, grad_far, lag)
    tokens = rows * lax.axis_size("seq")
    kernel_grad = totals[:, : 2 * lag] / math.sqrt(tokens * HEAD)
    gain_grad = totals[:, 2 * lag :].reshape(width) / math.sqrt(tokens)
    return (normed, gate_grad, value_grad, kernel_grad, gain_grad)


def solution(mesh):
    placed = (P("seq", "chan"), P("seq", "chan"), P("chan", None), P("chan"), P("seq", "chan"))
    return jax.shard_map(
        on_device,
        mesh=mesh,
        in_specs=placed,
        out_specs=(
            P("seq", "chan"),
            P("seq", "chan"),
            P("seq", "chan"),
            P("chan", None),
            P("chan"),
        ),
        check_vma=False,
    )
```

time: 976 us -> 206 us (0.21)
  local copies, waits for them, and re-layouts: 617 us -> 28 us
  waiting for transfers between devices: 166 us -> 63.1 us
  matrix products: 64.9 us -> 0 us
  Pallas kernels: 0 us -> 53.7 us
  blocking collectives: 46.5 us -> 2.45 us
  other arithmetic: 44.2 us -> 2.3 us
  starting transfers between devices: 13.5 us -> 54.9 us
  between operations: 14.6 us -> 0.85 us
    reshape x6 -> x4, local copies, waits for them, and re-layouts: 237 us -> 0.33 us  [the longest x2 0.17 us: bands(): rows.reshape(heads // 2, 2, length)]
    unnamed x51 -> x29, local copies, waits for them, and re-layouts: 231 us -> 20.4 us
    slice x6 -> x2, local copies, waits for them, and re-layouts: 133 us -> 4.73 us  [neighbours(): block[c * size:(c + 1) * size]]
    psum x1 -> x0, waiting for transfers between devices: 83.1 us -> none  [on_device(): kernel_total, gain_total = lax.psum((kernel_local, gain_local), 'seq')]
    dot_general x3 -> x0, matrix products: 64.9 us -> none  [the longest x1 31.6 us: on_device(): jnp.einsum('haw,hcpw->hcpa', forward_band, value_win, preferred_element_t...]
    pallas_call x0 -> x7, Pallas kernels: none -> 53.7 us  [the longest x1 13.6 us: kernel_grad_local(): pl.pallas_call(functools.partial(kernel_grad_body, slots), grid=(pairs,),...]
    psum x3 -> x1, blocking collectives: 46.5 us -> 2.45 us  [on_device(): sums = lax.psum(sums, 'chan')]
    ppermute x4 -> x20, starting transfers between devices: 13.5 us -> 54.9 us  [the longest x8 36.4 us: neighbours(): far = [lax.ppermute(piece, 'seq', relay) for piece in near]]
  transfers between devices with their start and end apart: 5 -> 20, of which waited for: 3 -> 11; matrix products, arithmetic and copies ran while one was open for 16% -> 3% of each run, Pallas kernels for 0% -> 3%
where the time goes in v1:
time: 206 us; the launch traced here: 205 us
  waiting for transfers between devices  63.1 us (31%)
  starting transfers between devices  54.9 us (27%)
  Pallas kernels  53.7 us (26%)
  local copies, waits for them, and re-layouts  28 us (14%)
  blocking collectives  2.45 us (1%)
  other arithmetic  2.3 us (1%)
    ppermute x8, waiting for transfers between devices, neighbours(): lax.ppermute(block[c * size:(c + 1) * size], 'seq', swap)  40 us
    ppermute x8, starting transfers between devices, neighbours(): far = [lax.ppermute(piece, 'seq', relay) for piece in near]  36.4 us
    unnamed x29, local copies, waits for them, and re-layouts  20.4 us
    ppermute x8, waiting for transfers between devices, neighbours(): far = [lax.ppermute(piece, 'seq', relay) for piece in near]  16.6 us
    pallas_call x1, Pallas kernels, kernel_grad_local(): pl.pallas_call(functools.partial(kernel_grad_body, slots), grid=(pairs,),...  13.6 us
    pallas_call x1, Pallas kernels, forward(): pl.pallas_call(functools.partial(forward_body, slots), grid=(width // LAN...  13.3 us
    pallas_call x1, Pallas kernels, value_grad_of(): pl.pallas_call(functools.partial(value_grad_body, slots), grid=(width //...  11 us
    pallas_call x2, Pallas kernels, norm_call(): pl.pallas_call(functools.partial(body, full_width), grid=(width // LANES,...  9.63 us
  transfers between devices with their start and end apart: 20, of which 11 were waited for; matrix products, arithmetic and copies ran while one was open for 3% of the time, Pallas kernels for 3%

profile of v1, /device:TPU:0, one launch (start us, length us, event | category | flops | bytes accessed | tf_op | source)
XLA Modules:
  0.0 205.3 jit_solution(14606143609141607827)
XLA Ops:
  7.5 10.6 %collective-permute-done.refs_0_ = bf16[256,1024]{1,0:T(8,128)(2,1)S(1)} collective-permute-done((bf16[256,1024]{1,0:T(8,128)(2,1)S(1)}, bf16[256,1024]{1,0:T(8,128)(2,1)S(1)}, u32[]{:S(2)}, u32[]{:S(2)}) %collective-permute-start) | collective-permute-done | bytes 524320 | tf_op jit(solution)/shard_map/ppermute | solution.py:380
  18.2 4.8 %collective-permute-start.4 = (bf16[256,1024]{1,0:T(8,128)(2,1)S(1)}, bf16[256,1024]{1,0:T(8,128)(2,1)}, u32[]{:S(2)}, u32[]{:S(2)}) collective-permute-start(bf16[256,1024]{1,0:T(8,128)(2,1)S(1)} %collective-permute-done.refs_0_), channel_id=1, source_target_pairs={{0,4},{4,8},{6,2},{8,12},{10,6},{12,16},{14,10},{16,20},{18,14},{2... | collective-permute-start | bytes 1572872 | tf_op jit(solution)/shard_map/ppermute | solution.py:382
  22.9 6.5 %collective-permute-done.1.refs_1_ = bf16[256,1024]{1,0:T(8,128)(2,1)S(1)} collective-permute-done((bf16[256,1024]{1,0:T(8,128)(2,1)S(1)}, bf16[256,1024]{1,0:T(8,128)(2,1)S(1)}, u32[]{:S(2)}, u32[]{:S(2)}) %collective-permute-start.1) | collective-permute-done | bytes 524320 | tf_op jit(solution)/shard_map/ppermute | solution.py:380
  29.4 4.8 %collective-permute-start.5 = (bf16[256,1024]{1,0:T(8,128)(2,1)S(1)}, bf16[256,1024]{1,0:T(8,128)(2,1)}, u32[]{:S(2)}, u32[]{:S(2)}) collective-permute-start(bf16[256,1024]{1,0:T(8,128)(2,1)S(1)} %collective-permute-done.1.refs_1_), channel_id=1, source_target_pairs={{0,4},{4,8},{6,2},{8,12},{10,6},{12,16},{14,10},{16,20},{18,14},{2... | collective-permute-start | bytes 1572872 | tf_op jit(solution)/shard_map/ppermute | solution.py:382
  34.2 6.5 %collective-permute-done.2.refs_2_ = bf16[256,1024]{1,0:T(8,128)(2,1)} collective-permute-done((bf16[256,1024]{1,0:T(8,128)(2,1)S(1)}, bf16[256,1024]{1,0:T(8,128)(2,1)}, u32[]{:S(2)}, u32[]{:S(2)}) %collective-permute-start.2) | collective-permute-done | bytes 524320 | tf_op jit(solution)/shard_map/ppermute | solution.py:380
  40.7 4.8 %collective-permute-start.6 = (bf16[256,1024]{1,0:T(8,128)(2,1)}, bf16[256,1024]{1,0:T(8,128)(2,1)}, u32[]{:S(2)}, u32[]{:S(2)}) collective-permute-start(bf16[256,1024]{1,0:T(8,128)(2,1)} %collective-permute-done.2.refs_2_), channel_id=1, source_target_pairs={{0,4},{4,8},{6,2},{8,12},{10,6},{12,16},{14,10},{16,20},{18,14},{2... | collective-permute-start | bytes 1572872 | tf_op jit(solution)/shard_map/ppermute | solution.py:382
  45.6 5.6 %collective-permute-done.3.refs_3_ = bf16[256,1024]{1,0:T(8,128)(2,1)} collective-permute-done((bf16[256,1024]{1,0:T(8,128)(2,1)S(1)}, bf16[256,1024]{1,0:T(8,128)(2,1)}, u32[]{:S(2)}, u32[]{:S(2)}) %collective-permute-start.3) | collective-permute-done | bytes 524320 | tf_op jit(solution)/shard_map/ppermute | solution.py:380
  51.2 4.5 %collective-permute-start.7 = (bf16[256,1024]{1,0:T(8,128)(2,1)}, bf16[256,1024]{1,0:T(8,128)(2,1)}, u32[]{:S(2)}, u32[]{:S(2)}) collective-permute-start(bf16[256,1024]{1,0:T(8,128)(2,1)} %collective-permute-done.3.refs_3_), channel_id=1, source_target_pairs={{0,4},{4,8},{6,2},{8,12},{10,6},{12,16},{14,10},{16,20},{18,14},{2... | collective-permute-start | bytes 1572872 | tf_op jit(solution)/shard_map/ppermute | solution.py:382
  60.2 3.8 %copy-done = bf16[16,128,2432]{2,1,0:T(8,128)(2,1)} copy-done((bf16[16,128,2432]{2,1,0:T(8,128)(2,1)}, bf16[16,128,2432]{2,1,0:T(8,128)(2,1)S(1)}, u32[]{:S(2)}) %copy-start) | copy-done | bytes 9961496
  68.6 13.3 %forward.1 = (f32[1024,1024]{1,0:T(8,128)S(1)}, f32[2,1024]{1,0:T(2,128)S(1)}) custom-call(s32[1]{0:T(128)} %bitcast.odd_ref_scalar, bf16[16,128,2432]{2,1,0:T(8,128)(2,1)} %copy-done, bf16[1024,1024]{1,0:T(8,128)(2,1)S(1)} %copy-done.10, bf16[256,1024]{1,0:T(8,128)(2,1)S(1)} %collective-permute-done.refs_0_, ...), custom_call_target="tpu_custom_call" | custom-call | flops 4831838208 | bytes 16777216 | tf_op jit(solution)/shard_map/forward/pallas_call | solution.py:184
  90.1 3.8 %mix_grad.1.own_ref.mix_ref = bf16[1024,1024]{1,0:T(8,128)(2,1)S(1)} custom-call(f32[2,1024]{1,0:T(2,128)S(1)} %psum.7.sums_ref, f32[1024,1024]{1,0:T(8,128)S(1)} %copy-done.9, bf16[1024,1024]{1,0:T(8,128)(2,1)S(1)} %copy-done.3, bf16[1024,1024]{1,0:T(8,128)(2,1)S(1)} %copy-done.5, f32[1,1024]{1,0:T(1,128)S(1)} %bitcast.3), custom_call_target="tpu_custom_call" | custom-call | flops 10485760 | bytes 12582912 | tf_op jit(solution)/shard_map/mix_grad/pallas_call | solution.py:257
  94.0 5.8 %norm.1 = (bf16[1024,1024]{1,0:T(8,128)(2,1)}, bf16[1024,1024]{1,0:T(8,128)(2,1)}, f32[1,1024]{1,0:T(1,128)S(1)}) custom-call(f32[2,1024]{1,0:T(2,128)S(1)} %psum.7.sums_ref, f32[1024,1024]{1,0:T(8,128)S(1)} %copy-done.9, bf16[1024,1024]{1,0:T(8,128)(2,1)S(1)} %copy-done.3, bf16[1024,1024]{1,0:T(8,128)(2,1)S(1)} %copy-done.5, f32[1,1024]{1,0:T(1,128)S(1)} %bitcast.4), custom_call_target="tpu_custom_call" | custom-call | flops 10485760 | bytes 12582912 | tf_op jit(solution)/shard_map/norm/pallas_call | solution.py:257
  99.8 13.6 %kernel_grad.1 = f32[8,2,2048]{2,1,0:T(2,128)S(1)} custom-call(s32[1]{0:T(128)} %bitcast.odd_ref_scalar, bf16[1024,1024]{1,0:T(8,128)(2,1)S(1)} %mix_grad.1.own_ref.mix_ref, bf16[1024,1024]{1,0:T(8,128)(2,1)S(1)} %copy-done.11, bf16[256,1024]{1,0:T(8,128)(2,1)S(1)} %collective-permute-done.refs_0_, bf16[256,1024]{1,0:T(8,128)(2,1)S(1)} %collective-permute-done.1.refs_1_, ...), custom_call_target="tpu_custom_call" | custom-call | flops 4831838208 | bytes 8388608 | tf_op jit(solution)/shard_map/kernel_grad/pallas_call | solution.py:316
  131.4 3.5 %collective-permute-done.18 = f32[16,2112]{1,0:T(8,128)S(1)} collective-permute-done((f32[16,2112]{1,0:T(8,128)S(1)}, f32[16,2112]{1,0:T(8,128)S(1)}, u32[]{:S(2)}, u32[]{:S(2)}) %collective-permute-start.18) | collective-permute-done | bytes 135200 | tf_op jit(solution)/shard_map/ppermute | solution.py:392
  140.9 3.8 %copy-done.1 = bf16[16,128,2432]{2,1,0:T(8,128)(2,1)} copy-done((bf16[16,128,2432]{2,1,0:T(8,128)(2,1)}, bf16[16,128,2432]{2,1,0:T(8,128)(2,1)S(1)}, u32[]{:S(2)}) %copy-start.1) | copy-done | bytes 9961496
  144.7 5.0 %collective-permute-start.12 = (bf16[256,1024]{1,0:T(8,128)(2,1)S(1)}, bf16[256,1024]{1,0:T(8,128)(2,1)}, u32[]{:S(2)}, u32[]{:S(2)}) collective-permute-start(bf16[256,1024]{1,0:T(8,128)(2,1)S(1)} %collective-permute-done.8.refs_0_), channel_id=1, source_target_pairs={{0,4},{4,8},{6,2},{8,12},{10,6},{12,16},{14,10},{16,20},{18,14},{2... | collective-permute-start | bytes 1572872 | tf_op jit(solution)/shard_map/ppermute | solution.py:382
  151.9 5.8 %collective-permute-done.10.refs_2_ = bf16[256,1024]{1,0:T(8,128)(2,1)} collective-permute-done((bf16[256,1024]{1,0:T(8,128)(2,1)}, bf16[256,1024]{1,0:T(8,128)(2,1)}, u32[]{:S(2)}, u32[]{:S(2)}) %collective-permute-start.10) | collective-permute-done | bytes 524320 | tf_op jit(solution)/shard_map/ppermute | solution.py:380
  157.7 5.2 %collective-permute-start.14 = (bf16[256,1024]{1,0:T(8,128)(2,1)}, bf16[256,1024]{1,0:T(8,128)(2,1)}, u32[]{:S(2)}, u32[]{:S(2)}) collective-permute-start(bf16[256,1024]{1,0:T(8,128)(2,1)} %collective-permute-done.10.refs_2_), channel_id=1, source_target_pairs={{0,4},{4,8},{6,2},{8,12},{10,6},{12,16},{14,10},{16,20},{18,14},{2... | collective-permute-start | bytes 1572872 | tf_op jit(solution)/shard_map/ppermute | solution.py:382
  162.9 5.0 %collective-permute-done.11.refs_3_ = bf16[256,1024]{1,0:T(8,128)(2,1)} collective-permute-done((bf16[256,1024]{1,0:T(8,128)(2,1)}, bf16[256,1024]{1,0:T(8,128)(2,1)}, u32[]{:S(2)}, u32[]{:S(2)}) %collective-permute-start.11) | collective-permute-done | bytes 524320 | tf_op jit(solution)/shard_map/ppermute | solution.py:380
  167.9 5.1 %collective-permute-start.15 = (bf16[256,1024]{1,0:T(8,128)(2,1)}, bf16[256,1024]{1,0:T(8,128)(2,1)}, u32[]{:S(2)}, u32[]{:S(2)}) collective-permute-start(bf16[256,1024]{1,0:T(8,128)(2,1)} %collective-permute-done.11.refs_3_), channel_id=1, source_target_pairs={{0,4},{4,8},{6,2},{8,12},{10,6},{12,16},{14,10},{16,20},{18,14},{2... | collective-permute-start | bytes 1572872 | tf_op jit(solution)/shard_map/ppermute | solution.py:382
  175.3 8.6 %collective-permute-done.14.refs_6_ = bf16[256,1024]{1,0:T(8,128)(2,1)} collective-permute-done((bf16[256,1024]{1,0:T(8,128)(2,1)}, bf16[256,1024]{1,0:T(8,128)(2,1)}, u32[]{:S(2)}, u32[]{:S(2)}) %collective-permute-start.14) | collective-permute-done | bytes 524320 | tf_op jit(solution)/shard_map/ppermute | solution.py:382
  183.9 6.6 %collective-permute-done.15.refs_7_ = bf16[256,1024]{1,0:T(8,128)(2,1)} collective-permute-done((bf16[256,1024]{1,0:T(8,128)(2,1)}, bf16[256,1024]{1,0:T(8,128)(2,1)}, u32[]{:S(2)}, u32[]{:S(2)}) %collective-permute-start.15) | collective-permute-done | bytes 524320 | tf_op jit(solution)/shard_map/ppermute | solution.py:382
  190.5 3.8 %copy-done.2 = bf16[16,128,2432]{2,1,0:T(8,128)(2,1)S(1)} copy-done((bf16[16,128,2432]{2,1,0:T(8,128)(2,1)S(1)}, bf16[16,128,2432]{2,1,0:T(8,128)(2,1)}, u32[]{:S(2)}) %copy-start.2) | copy-done | bytes 9961496
  194.3 11.0 %value_grad.1 = bf16[1024,1024]{1,0:T(8,128)(2,1)} custom-call(s32[1]{0:T(128)} %bitcast.odd_ref_scalar, bf16[16,128,2432]{2,1,0:T(8,128)(2,1)S(1)} %copy-done.2, bf16[1024,1024]{1,0:T(8,128)(2,1)S(1)} %copy-done.7, bf16[256,1024]{1,0:T(8,128)(2,1)S(1)} %collective-permute-done.8.refs_0_, bf16[256,1024]{1,0:T(8,128)(2,1)S(1)} %collective-permute-done.9.refs_1_, ...), custom_call_target="tpu_custom_call" | custom-call | flops 4831838208 | bytes 12582912 | tf_op jit(solution)/shard_map/value_grad/pallas_call | solution.py:356
  (72 shorter events, 52.7 us)
Async XLA Ops:
  0.6 55.0 %copy-start.13 = (bf16[16,2048]{1,0:T(8,128)(2,1)S(1)}, bf16[16,2048]{1,0:T(8,128)(2,1)}, u32[]{:S(2)}) copy-start(bf16[16,2048]{1,0:T(8,128)(2,1)} %param.7) | copy-start | bytes 196612
  2.4 15.8 %collective-permute-start = (bf16[256,1024]{1,0:T(8,128)(2,1)S(1)}, bf16[256,1024]{1,0:T(8,128)(2,1)S(1)}, u32[]{:S(2)}, u32[]{:S(2)}) collective-permute-start(bf16[256,1024]{1,0:T(8,128)(2,1)S(1)} %get-tuple-element.22), channel_id=1, source_target_pairs={{0,2},{2,0},{4,6},{6,4},{8,10},{10,8},{12,14},{14,12},{16,18},{18,... | collective-permute-start | bytes 1572872 | tf_op jit(solution)/shard_map/ppermute | solution.py:380
  5.4 24.0 %collective-permute-start.1 = (bf16[256,1024]{1,0:T(8,128)(2,1)S(1)}, bf16[256,1024]{1,0:T(8,128)(2,1)S(1)}, u32[]{:S(2)}, u32[]{:S(2)}) collective-permute-start(bf16[256,1024]{1,0:T(8,128)(2,1)S(1)} %get-tuple-element.21), channel_id=1, source_target_pairs={{0,2},{2,0},{4,6},{6,4},{8,10},{10,8},{12,14},{14,12},{16,18},{18,... | collective-permute-start | bytes 1572872 | tf_op jit(solution)/shard_map/ppermute | solution.py:380
  5.5 35.2 %collective-permute-start.2 = (bf16[256,1024]{1,0:T(8,128)(2,1)S(1)}, bf16[256,1024]{1,0:T(8,128)(2,1)}, u32[]{:S(2)}, u32[]{:S(2)}) collective-permute-start(bf16[256,1024]{1,0:T(8,128)(2,1)S(1)} %get-tuple-element.20), channel_id=1, source_target_pairs={{0,2},{2,0},{4,6},{6,4},{8,10},{10,8},{12,14},{14,12},{16,18},{18,... | collective-permute-start | bytes 1572872 | tf_op jit(solution)/shard_map/ppermute | solution.py:380
  7.4 43.7 %collective-permute-start.3 = (bf16[256,1024]{1,0:T(8,128)(2,1)S(1)}, bf16[256,1024]{1,0:T(8,128)(2,1)}, u32[]{:S(2)}, u32[]{:S(2)}) collective-permute-start(bf16[256,1024]{1,0:T(8,128)(2,1)S(1)} %get-tuple-element.19), channel_id=1, source_target_pairs={{0,2},{2,0},{4,6},{6,4},{8,10},{10,8},{12,14},{14,12},{16,18},{18,... | collective-permute-start | bytes 1572872 | tf_op jit(solution)/shard_map/ppermute | solution.py:380
  18.2 45.9 %collective-permute-start.4 = (bf16[256,1024]{1,0:T(8,128)(2,1)S(1)}, bf16[256,1024]{1,0:T(8,128)(2,1)}, u32[]{:S(2)}, u32[]{:S(2)}) collective-permute-start(bf16[256,1024]{1,0:T(8,128)(2,1)S(1)} %collective-permute-done.refs_0_), channel_id=1, source_target_pairs={{0,4},{4,8},{6,2},{8,12},{10,6},{12,16},{14,10},{16,20},{18,14},{2... | collective-permute-start | bytes 1572872 | tf_op jit(solution)/shard_map/ppermute | solution.py:382
  29.4 34.6 %collective-permute-start.5 = (bf16[256,1024]{1,0:T(8,128)(2,1)S(1)}, bf16[256,1024]{1,0:T(8,128)(2,1)}, u32[]{:S(2)}, u32[]{:S(2)}) collective-permute-start(bf16[256,1024]{1,0:T(8,128)(2,1)S(1)} %collective-permute-done.1.refs_1_), channel_id=1, source_target_pairs={{0,4},{4,8},{6,2},{8,12},{10,6},{12,16},{14,10},{16,20},{18,14},{2... | collective-permute-start | bytes 1572872 | tf_op jit(solution)/shard_map/ppermute | solution.py:382
  40.7 23.3 %collective-permute-start.6 = (bf16[256,1024]{1,0:T(8,128)(2,1)}, bf16[256,1024]{1,0:T(8,128)(2,1)}, u32[]{:S(2)}, u32[]{:S(2)}) collective-permute-start(bf16[256,1024]{1,0:T(8,128)(2,1)} %collective-permute-done.2.refs_2_), channel_id=1, source_target_pairs={{0,4},{4,8},{6,2},{8,12},{10,6},{12,16},{14,10},{16,20},{18,14},{2... | collective-permute-start | bytes 1572872 | tf_op jit(solution)/shard_map/ppermute | solution.py:382
  51.2 14.3 %collective-permute-start.7 = (bf16[256,1024]{1,0:T(8,128)(2,1)}, bf16[256,1024]{1,0:T(8,128)(2,1)}, u32[]{:S(2)}, u32[]{:S(2)}) collective-permute-start(bf16[256,1024]{1,0:T(8,128)(2,1)} %collective-permute-done.3.refs_3_), channel_id=1, source_target_pairs={{0,4},{4,8},{6,2},{8,12},{10,6},{12,16},{14,10},{16,20},{18,14},{2... | collective-permute-start | bytes 1572872 | tf_op jit(solution)/shard_map/ppermute | solution.py:382
  57.0 8.4 %copy-start.3 = (bf16[1024,1024]{1,0:T(8,128)(2,1)S(1)}, bf16[1024,1024]{1,0:T(8,128)(2,1)}, u32[]{:S(2)}) copy-start(bf16[1024,1024]{1,0:T(8,128)(2,1)} %gate_ref.3) | copy-start | bytes 6291460
  57.0 8.4 %copy-start.12 = (f32[1024]{0:T(1024)S(1)}, f32[1024]{0:T(1024)}, u32[]{:S(2)}) copy-start(f32[1024]{0:T(1024)} %param.8) | copy-start | bytes 12292
  114.7 9.5 %collective-permute-start.16 = (f32[16,2112]{1,0:T(8,128)S(1)}, f32[16,2112]{1,0:T(8,128)S(1)}, u32[]{:S(2)}, u32[]{:S(2)}) collective-permute-start(f32[16,2112]{1,0:T(8,128)S(1)} %constant_dynamic-update-slice_fusion), channel_id=1, source_target_pairs={{0,2},{2,0},{4,6},{6,4},{8,10},{10,8},{12,14},{14,12},{16,18},{18,... | collective-permute-start | bytes 405512 | tf_op jit(solution)/shard_map/ppermute | solution.py:392
  120.1 24.6 %collective-permute-start.8 = (bf16[256,1024]{1,0:T(8,128)(2,1)}, bf16[256,1024]{1,0:T(8,128)(2,1)S(1)}, u32[]{:S(2)}, u32[]{:S(2)}) collective-permute-start(bf16[256,1024]{1,0:T(8,128)(2,1)} %get-tuple-element.18), channel_id=1, source_target_pairs={{0,2},{2,0},{4,6},{6,4},{8,10},{10,8},{12,14},{14,12},{16,18},{18,... | collective-permute-start | bytes 1572872 | tf_op jit(solution)/shard_map/ppermute | solution.py:380
  120.1 29.6 %collective-permute-start.9 = (bf16[256,1024]{1,0:T(8,128)(2,1)}, bf16[256,1024]{1,0:T(8,128)(2,1)S(1)}, u32[]{:S(2)}, u32[]{:S(2)}) collective-permute-start(bf16[256,1024]{1,0:T(8,128)(2,1)} %get-tuple-element.17), channel_id=1, source_target_pairs={{0,2},{2,0},{4,6},{6,4},{8,10},{10,8},{12,14},{14,12},{16,18},{18,... | collective-permute-start | bytes 1572872 | tf_op jit(solution)/shard_map/ppermute | solution.py:380
  122.2 35.6 %collective-permute-start.10 = (bf16[256,1024]{1,0:T(8,128)(2,1)}, bf16[256,1024]{1,0:T(8,128)(2,1)}, u32[]{:S(2)}, u32[]{:S(2)}) collective-permute-start(bf16[256,1024]{1,0:T(8,128)(2,1)} %get-tuple-element.16), channel_id=1, source_target_pairs={{0,2},{2,0},{4,6},{6,4},{8,10},{10,8},{12,14},{14,12},{16,18},{18,... | collective-permute-start | bytes 1572872 | tf_op jit(solution)/shard_map/ppermute | solution.py:380
  122.2 45.7 %collective-permute-start.11 = (bf16[256,1024]{1,0:T(8,128)(2,1)}, bf16[256,1024]{1,0:T(8,128)(2,1)}, u32[]{:S(2)}, u32[]{:S(2)}) collective-permute-start(bf16[256,1024]{1,0:T(8,128)(2,1)} %get-tuple-element.15), channel_id=1, source_target_pairs={{0,2},{2,0},{4,6},{6,4},{8,10},{10,8},{12,14},{14,12},{16,18},{18,... | collective-permute-start | bytes 1572872 | tf_op jit(solution)/shard_map/ppermute | solution.py:380
  124.2 5.5 %collective-permute-start.17 = (f32[16,2112]{1,0:T(8,128)S(1)}, f32[16,2112]{1,0:T(8,128)S(1)}, u32[]{:S(2)}, u32[]{:S(2)}) collective-permute-start(f32[16,2112]{1,0:T(8,128)S(1)} %add.23), channel_id=1, source_target_pairs={{0,4},{2,6},{4,0},{6,2},{8,12},{10,14},{12,8},{14,10},{16,20},{18,... | collective-permute-start | bytes 405512 | tf_op jit(solution)/shard_map/ppermute | solution.py:392
  129.7 5.1 %collective-permute-start.18 = (f32[16,2112]{1,0:T(8,128)S(1)}, f32[16,2112]{1,0:T(8,128)S(1)}, u32[]{:S(2)}, u32[]{:S(2)}) collective-permute-start(f32[16,2112]{1,0:T(8,128)S(1)} %add.24), channel_id=1, source_target_pairs={{0,8},{2,10},{4,12},{6,14},{8,0},{10,2},{12,4},{14,6},{16,24},{18,... | collective-permute-start | bytes 405512 | tf_op jit(solution)/shard_map/ppermute | solution.py:392
  134.9 38.1 %collective-permute-start.19 = (f32[16,2112]{1,0:T(8,128)S(1)}, f32[16,2112]{1,0:T(8,128)}, u32[]{:S(2)}, u32[]{:S(2)}) collective-permute-start(f32[16,2112]{1,0:T(8,128)S(1)} %add.25), channel_id=1, source_target_pairs={{0,16},{2,18},{4,20},{6,22},{8,24},{10,26},{12,28},{14,30},{16,0},... | collective-permute-start | bytes 405512 | tf_op jit(solution)/shard_map/ppermute | solution.py:392
  137.7 52.8 %copy-start.7 = (bf16[1024,1024]{1,0:T(8,128)(2,1)S(1)}, bf16[1024,1024]{1,0:T(8,128)(2,1)}, u32[]{:S(2)}) copy-start(bf16[1024,1024]{1,0:T(8,128)(2,1)} %copy-done.6) | copy-start | bytes 6291460
  144.7 30.6 %collective-permute-start.12 = (bf16[256,1024]{1,0:T(8,128)(2,1)S(1)}, bf16[256,1024]{1,0:T(8,128)(2,1)}, u32[]{:S(2)}, u32[]{:S(2)}) collective-permute-start(bf16[256,1024]{1,0:T(8,128)(2,1)S(1)} %collective-permute-done.8.refs_0_), channel_id=1, source_target_pairs={{0,4},{4,8},{6,2},{8,12},{10,6},{12,16},{14,10},{16,20},{18,14},{2... | collective-permute-start | bytes 1572872 | tf_op jit(solution)/shard_map/ppermute | solution.py:382
  149.7 25.5 %collective-permute-start.13 = (bf16[256,1024]{1,0:T(8,128)(2,1)S(1)}, bf16[256,1024]{1,0:T(8,128)(2,1)}, u32[]{:S(2)}, u32[]{:S(2)}) collective-permute-start(bf16[256,1024]{1,0:T(8,128)(2,1)S(1)} %collective-permute-done.9.refs_1_), channel_id=1, source_target_pairs={{0,4},{4,8},{6,2},{8,12},{10,6},{12,16},{14,10},{16,20},{18,14},{2... | collective-permute-start | bytes 1572872 | tf_op jit(solution)/shard_map/ppermute | solution.py:382
  157.7 26.2 %collective-permute-start.14 = (bf16[256,1024]{1,0:T(8,128)(2,1)}, bf16[256,1024]{1,0:T(8,128)(2,1)}, u32[]{:S(2)}, u32[]{:S(2)}) collective-permute-start(bf16[256,1024]{1,0:T(8,128)(2,1)} %collective-permute-done.10.refs_2_), channel_id=1, source_target_pairs={{0,4},{4,8},{6,2},{8,12},{10,6},{12,16},{14,10},{16,20},{18,14},{2... | collective-permute-start | bytes 1572872 | tf_op jit(solution)/shard_map/ppermute | solution.py:382
  167.9 22.6 %collective-permute-start.15 = (bf16[256,1024]{1,0:T(8,128)(2,1)}, bf16[256,1024]{1,0:T(8,128)(2,1)}, u32[]{:S(2)}, u32[]{:S(2)}) collective-permute-start(bf16[256,1024]{1,0:T(8,128)(2,1)} %collective-permute-done.11.refs_3_), channel_id=1, source_target_pairs={{0,4},{4,8},{6,2},{8,12},{10,6},{12,16},{14,10},{16,20},{18,14},{2... | collective-permute-start | bytes 1572872 | tf_op jit(solution)/shard_map/ppermute | solution.py:382
  (10 other events, 32.0 us)

commit v2 on v1

v2 whole, which is shorter than its diff:
```python
import functools
import math

import jax
import jax.numpy as jnp
from jax import lax
from jax.experimental import pallas as pl
from jax.experimental.pallas import tpu as pltpu
from jax.sharding import PartitionSpec as P

norm_eps = 1e-06
TILE = 256
LANES = 128
HEAD = 64
VALUE_CHUNKS = 8
GRAD_CHUNKS = 4
MIB = 1 << 20


def params(mib):
    return pltpu.CompilerParams(
        vmem_limit_bytes=mib * MIB, dimension_semantics=("arbitrary",)
    )


def cost(flops, moved):
    return pl.CostEstimate(flops=flops, bytes_accessed=moved, transcendentals=0)


def lane_iota(rows):
    return lax.broadcasted_iota(jnp.int32, (rows, LANES), 1)


def slab(first=0):
    return pl.ds(pl.multiple_of((first + pl.program_id(0)) * LANES, LANES), LANES)


VMEM = pl.BlockSpec(memory_space=pltpu.VMEM)


def held(*arrays):
    return [pltpu.with_memory_space_constraint(array, pltpu.VMEM) for array in arrays]


def after(value, *others):
    return lax.optimization_barrier((value, *others))[0]


def band_body(row_ref, band_ref):
    tiles = row_ref.shape[2] // LANES
    step = pl.program_id(0)
    upper = lane_iota(LANES) >= lax.broadcasted_iota(jnp.int32, (LANES, LANES), 0)
    for half in range(2):
        head = 2 * step + half
        before = jnp.zeros((LANES, LANES), jnp.float32)
        band_ref[head, :, :LANES] = before.astype(band_ref.dtype)
        for tile in range(tiles):
            segment = row_ref[step, half : half + 1, tile * LANES : (tile + 1) * LANES]
            turned = pltpu.roll(
                jnp.broadcast_to(segment, (LANES, LANES)), 0, 1, stride=1, stride_axis=0
            )
            cell = jnp.where(upper, turned, before)
            band_ref[head, :, (tile + 1) * LANES : (tile + 2) * LANES] = cell.astype(
                band_ref.dtype
            )
            before = turned


def band_rows(taps, low, high):
    heads = taps.shape[0]
    return jnp.pad(taps, ((0, 0), (low, high))).reshape(heads // 2, 2, -1)


def bands(rows):
    heads, length = 2 * rows.shape[0], rows.shape[2]
    return pl.pallas_call(
        band_body,
        grid=(heads // 2,),
        in_specs=[VMEM],
        out_specs=VMEM,
        out_shape=pltpu.VMEM((heads, LANES, length + LANES), jnp.bfloat16),
        compiler_params=params(4),
        cost_estimate=cost(heads * LANES * length, 2 * heads * LANES * length),
        name="bands",
    )(*held(rows))


def blocks_of(refs, first=0):
    pieces = []
    for ref in refs:
        size = min(TILE, ref.shape[0])
        pieces += [ref[row : row + size, slab(first)] for row in range(0, ref.shape[0], size)]
    per = TILE // pieces[0].shape[0]
    return [
        pieces[at] if per == 1 else jnp.concatenate(pieces[at : at + per], axis=0)
        for at in range(0, len(pieces), per)
    ]


def layout_scratch(rows, lag):
    wide = (rows + 2 * lag) // TILE * HEAD
    return [
        pltpu.VMEM((2, TILE, wide), jnp.bfloat16),
        pltpu.VMEM((2, TILE, wide - LANES), jnp.bfloat16),
    ]


def lay_out(blocks, even_ref, odd_ref):
    low = lane_iota(TILE) < HEAD
    turned = [pltpu.roll(block, HEAD, 1) for block in blocks]
    for tile in range(len(blocks) // 2):
        cols = slice(tile * LANES, (tile + 1) * LANES)
        first, second = 2 * tile, 2 * tile + 1
        even_ref[0, :, cols] = jnp.where(low, blocks[first], turned[second])
        even_ref[1, :, cols] = jnp.where(low, turned[first], blocks[second])
        if odd_ref is not None and second + 1 < len(blocks):
            odd_ref[0, :, cols] = jnp.where(low, blocks[second], turned[second + 1])
            odd_ref[1, :, cols] = jnp.where(low, turned[second], blocks[second + 1])


def window(even_ref, odd_ref, head, start, width):
    if start % 2 == 0:
        return even_ref[head, :, start * HEAD : start * HEAD + width]
    return odd_ref[head, :, (start - 1) * HEAD : (start - 1) * HEAD + width]


def extended(own_refs, near_refs, far_refs, first=0):
    odd_dev = lax.axis_index("seq") % 2 == 1
    near, far = blocks_of(near_refs, first), blocks_of(far_refs, first)
    left = [jnp.where(odd_dev, n, f) for n, f in zip(near, far)]
    right = [jnp.where(odd_dev, f, n) for n, f in zip(near, far)]
    return left + blocks_of(own_refs, first) + right


def band_product(band_ref, band_head, even_ref, odd_ref, head, slots, width):
    span = slots * TILE
    tile = jnp.concatenate(
        [band_ref[band_head, :, LANES : LANES + span], band_ref[band_head, :, :span]], axis=0
    )
    data = jnp.concatenate(
        [window(even_ref, odd_ref, head, slot, width) for slot in range(slots)], axis=0
    )
    return jnp.dot(tile, data, preferred_element_type=jnp.float32)


def token_blocks(first, second):
    low = lane_iota(TILE) < HEAD
    blocks = []
    for tile in range(first.shape[1] // LANES):
        cols = slice(tile * LANES, (tile + 1) * LANES)
        one, two = first[:, cols], second[:, cols]
        blocks.append(jnp.where(low, one, pltpu.roll(two, HEAD, 1)))
        blocks.append(jnp.where(low, pltpu.roll(one, HEAD, 1), two))
    return blocks


def product_flops(rows, width, lag):
    return 2 * (width // HEAD) * TILE * (TILE + 2 * lag) * rows // TILE * HEAD


def forward_body(slots, sizes, band_ref, *refs):
    own_refs, refs = refs[: sizes[0]], refs[sizes[0] :]
    near_refs, refs = refs[: sizes[1]], refs[sizes[1] :]
    far_refs, refs = refs[: sizes[2]], refs[sizes[2] :]
    gate_ref, grad_ref, gain_ref, mixed_ref, sums_ref = refs[:5]
    even_ref, odd_ref, square_ref, inner_ref = refs[5:]
    step = pl.program_id(0)

    @pl.when(step == 0)
    def _():
        square_ref[...] = jnp.zeros_like(square_ref)
        inner_ref[...] = jnp.zeros_like(inner_ref)

    rows = mixed_ref.shape[0]
    width = rows // TILE * HEAD
    blocks = extended(own_refs, near_refs, far_refs)
    lay_out(blocks, even_ref, odd_ref)
    results = [
        band_product(band_ref, 2 * step + half, even_ref, odd_ref, half, slots, width)
        for half in range(2)
    ]
    for index, mixed in enumerate(token_blocks(*results)):
        at = slice(index * TILE, (index + 1) * TILE)
        mixed_ref[at, slab()] = mixed
        hidden = gate_ref[at, slab()].astype(jnp.float32) * mixed
        weighted = gain_ref[:, slab()] * grad_ref[at, slab()].astype(jnp.float32)
        square_ref[at, :] += hidden * hidden
        inner_ref[at, :] += weighted * hidden

    @pl.when(step == pl.num_programs(0) - 1)
    def _():
        for at in range(0, rows, LANES):
            cols = slice(at, at + LANES)
            sums_ref[0:1, cols] = jnp.sum(square_ref[cols, :].T, axis=0, keepdims=True)
            sums_ref[1:2, cols] = jnp.sum(inner_ref[cols, :].T, axis=0, keepdims=True)


def forward(band, own, near, far, gate, grad, gain, lag):
    rows, width = gate.shape
    slots = 1 + 2 * lag // TILE
    operands = held(band, *own, *near, *far, gate, grad, gain)
    sizes = (len(own), len(near), len(far))
    return pl.pallas_call(
        functools.partial(forward_body, slots, sizes),
        grid=(width // LANES,),
        in_specs=[VMEM] * len(operands),
        out_specs=[VMEM] * 2,
        out_shape=[
            pltpu.VMEM((rows, width), jnp.float32),
            pltpu.VMEM((2, rows), jnp.float32),
        ],
        scratch_shapes=layout_scratch(rows, lag)
        + [pltpu.VMEM((rows, LANES), jnp.float32)] * 2,
        compiler_params=params(10),
        cost_estimate=cost(product_flops(rows, width, lag), 16 * rows * width),
        name="forward",
    )(*operands)


def token_columns(full_width, sums_ref, at):
    cols = slice(at, at + LANES)
    scale = lax.rsqrt(sums_ref[0:1, cols] / full_width + norm_eps)
    pull = scale * scale * sums_ref[1:2, cols] / full_width
    return (
        jnp.broadcast_to(scale, (LANES, LANES)).T,
        jnp.broadcast_to(pull, (LANES, LANES)).T,
    )


def mix_grad_body(full_width, sums_ref, mixed_ref, gate_ref, grad_ref, gain_ref, *out_refs):
    size = out_refs[0].shape[0]
    for at in range(0, mixed_ref.shape[0], LANES):
        scale, pull = token_columns(full_width, sums_ref, at)
        rows = slice(at, at + LANES)
        out_ref, start = out_refs[at // size], at % size
        for lane in range(0, mixed_ref.shape[1], LANES):
            cols = slice(lane, lane + LANES)
            gate = gate_ref[rows, cols].astype(jnp.float32)
            hidden = gate * mixed_ref[rows, cols]
            weighted = gain_ref[:, cols] * grad_ref[rows, cols].astype(jnp.float32)
            hidden_grad = scale * (weighted - hidden * pull)
            out_ref[start : start + LANES, cols] = (hidden_grad * gate).astype(out_ref.dtype)


def mix_grad_of(full_width, chunks, sums, mixed, gate, grad, gain):
    rows, width = mixed.shape
    operands = held(sums, mixed, gate, grad, gain)
    return pl.pallas_call(
        functools.partial(mix_grad_body, full_width),
        in_specs=[VMEM] * len(operands),
        out_specs=[VMEM] * chunks,
        out_shape=[pltpu.VMEM((rows // chunks, width), jnp.bfloat16)] * chunks,
        compiler_params=pltpu.CompilerParams(vmem_limit_bytes=4 * MIB),
        cost_estimate=cost(10 * rows * width, 10 * rows * width),
        name="mix_grad",
    )(*operands)


def norm_body(full_width, sums_ref, mixed_ref, gate_ref, grad_ref, gain_ref, *refs):
    normed_ref, gate_grad_ref, gain_grad_ref, total_ref = refs
    step = pl.program_id(0)

    @pl.when(step == 0)
    def _():
        total_ref[...] = jnp.zeros_like(total_ref)

    tokens = pl.ds(pl.multiple_of(step * LANES, LANES), LANES)
    scale_row = lax.rsqrt(sums_ref[0:1, tokens] / full_width + norm_eps)
    pull_row = scale_row * scale_row * sums_ref[1:2, tokens] / full_width
    scale = jnp.broadcast_to(scale_row, (LANES, LANES)).T
    pull = jnp.broadcast_to(pull_row, (LANES, LANES)).T
    for lane in range(0, mixed_ref.shape[1], LANES):
        cols = slice(lane, lane + LANES)
        gain = gain_ref[:, cols]
        gate = gate_ref[tokens, cols].astype(jnp.float32)
        mixed = mixed_ref[tokens, cols]
        grad = grad_ref[tokens, cols].astype(jnp.float32)
        hidden = gate * mixed
        scaled = hidden * scale
        normed_ref[:, cols] = (scaled * gain).astype(normed_ref.dtype)
        hidden_grad = scale * (gain * grad - hidden * pull)
        gate_grad_ref[:, cols] = (hidden_grad * mixed).astype(gate_grad_ref.dtype)
        total_ref[:, cols] += jnp.sum((grad * scaled).reshape(LANES // 8, 8, LANES), axis=0)

    @pl.when(step == pl.num_programs(0) - 1)
    def _():
        gain_grad_ref[...] = jnp.sum(total_ref[...], axis=0, keepdims=True)


def norm(full_width, sums, mixed, gate, grad, gain):
    rows, width = mixed.shape
    operands = held(sums, mixed, gate, grad, gain)
    big = jax.ShapeDtypeStruct((rows, width), jnp.bfloat16)
    return pl.pallas_call(
        functools.partial(norm_body, full_width),
        grid=(rows // LANES,),
        in_specs=[VMEM] * len(operands),
        out_specs=[pl.BlockSpec((LANES, width), lambda g: (g, 0))] * 2 + [VMEM],
        out_shape=[big, big, pltpu.VMEM((1, width), jnp.float32)],
        scratch_shapes=[pltpu.VMEM((8, width), jnp.float32)],
        compiler_params=params(6),
        cost_estimate=cost(14 * rows * width, 12 * rows * width),
        name="norm",
    )(*operands)


def kernel_grad_body(first, slots, sizes, gain_ref, *refs):
    own_refs, refs = refs[: sizes[0]], refs[sizes[0] :]
    near_refs, refs = refs[: sizes[1]], refs[sizes[1] :]
    far_refs, refs = refs[: sizes[2]], refs[sizes[2] :]
    mix_refs, (out_ref, even_ref, odd_ref, mix_even_ref, cells_ref) = refs[:-5], refs[-5:]
    step = pl.program_id(0)
    blocks = extended(own_refs, near_refs, far_refs, first)
    lay_out(blocks, even_ref, odd_ref)
    blocks = blocks_of(mix_refs, first)
    lay_out(blocks, mix_even_ref, None)
    width = len(blocks) * HEAD
    span = cells_ref.shape[1]
    lags = span - LANES
    gains = gain_ref[:, slab(first)]
    for half in range(2):
        mix = mix_even_ref[half]
        carry = None
        for lag_slot in range(slots):
            cross = lax.dot_general(
                window(even_ref, odd_ref, half, slots - 1 - lag_slot, width),
                mix,
                (((1,), (1,)), ((), ())),
                preferred_element_type=jnp.float32,
            )
            at = 2 * lag_slot * LANES
            upper, lower = cross[:LANES], cross[LANES:]
            if carry is not None:
                cells_ref[:, at - LANES : at] = carry + lower[:, :LANES]
            cells_ref[:, at : at + LANES] = upper[:, :LANES] + lower[:, LANES:]
            carry = upper[:, LANES:]
        total = cells_ref[0:8, :]
        for group in range(1, LANES // 8):
            total += pltpu.roll(cells_ref[8 * group : 8 * group + 8, :], span - 8 * group, 1)
        row = lax.broadcasted_iota(jnp.int32, (8, span), 0)
        for bit in (1, 2, 4):
            total = jnp.where((row & bit) != 0, pltpu.roll(total, span - bit, 1), total)
        sums = jnp.concatenate(
            [
                jnp.sum(total, axis=0, keepdims=True)[:, :lags],
                gains if half == 0 else pltpu.roll(gains, HEAD, 1),
            ],
            axis=1,
        )
        own_row = lax.broadcasted_iota(jnp.int32, out_ref.shape, 0) == 2 * step + half
        out_ref[...] = jnp.where(own_row, sums, out_ref[...])


def kernel_grad_local(first, pairs, gain_sums, own, near, far, mix_grad, lag):
    rows, width = sum(chunk.shape[0] for chunk in mix_grad), 2 * pairs * HEAD
    slots = 1 + 2 * lag // TILE
    operands = held(gain_sums, *own, *near, *far, *mix_grad)
    sizes = (len(own), len(near), len(far))
    return pl.pallas_call(
        functools.partial(kernel_grad_body, first, slots, sizes),
        grid=(pairs,),
        in_specs=[VMEM] * len(operands),
        out_specs=VMEM,
        out_shape=pltpu.VMEM((2 * pairs, 2 * lag + LANES), jnp.float32),
        scratch_shapes=layout_scratch(rows, lag)
        + [
            pltpu.VMEM((2, TILE, rows // TILE * HEAD), jnp.bfloat16),
            pltpu.VMEM((LANES, 2 * lag + LANES), jnp.float32),
        ],
        compiler_params=params(10),
        cost_estimate=cost(product_flops(rows, width, lag), 8 * rows * width),
        name="kernel_grad",
    )(*operands)


def value_grad_body(slots, sizes, band_ref, *refs):
    own_refs, refs = refs[: sizes[0]], refs[sizes[0] :]
    near_refs, refs = refs[: sizes[1]], refs[sizes[1] :]
    far_refs, (out_ref, even_ref, odd_ref) = refs[: sizes[2]], refs[sizes[2] :]
    step = pl.program_id(0)
    width = out_ref.shape[0] // TILE * HEAD
    blocks = extended(own_refs, near_refs, far_refs)
    lay_out(blocks, even_ref, odd_ref)
    results = [
        band_product(band_ref, 2 * step + half, even_ref, odd_ref, half, slots, width)
        for half in range(2)
    ]
    for index, block in enumerate(token_blocks(*results)):
        out_ref[index * TILE : (index + 1) * TILE, :] = block.astype(out_ref.dtype)


def value_grad_of(band, own, near, far, lag):
    rows, width = sum(chunk.shape[0] for chunk in own), own[0].shape[1]
    slots = 1 + 2 * lag // TILE
    operands = held(band, *own, *near, *far)
    sizes = (len(own), len(near), len(far))
    return pl.pallas_call(
        functools.partial(value_grad_body, slots, sizes),
        grid=(width // LANES,),
        in_specs=[VMEM] * len(operands),
        out_specs=pl.BlockSpec((rows, LANES), lambda g: (0, g)),
        out_shape=jax.ShapeDtypeStruct((rows, width), jnp.bfloat16),
        scratch_shapes=layout_scratch(rows, lag),
        compiler_params=params(10),
        cost_estimate=cost(product_flops(rows, width, lag), 12 * rows * width),
        name="value_grad",
    )(*operands)


def swapped(chunk):
    count = lax.axis_size("seq")
    return lax.ppermute(chunk, "seq", [(i, i ^ 1) for i in range(count)])


def relayed(chunk):
    count = lax.axis_size("seq")
    pairs = [(i, i + 2) if i % 2 == 0 else (i, i - 2) for i in range(count)]
    return lax.ppermute(chunk, "seq", [(i, j) for i, j in pairs if 0 <= j < count])


def sum_over(value, axis):
    count = lax.axis_size(axis)
    if count & (count - 1):
        return lax.psum(value, axis)
    for bit in range(count.bit_length() - 1):
        value += lax.ppermute(value, axis, [(i, i ^ (1 << bit)) for i in range(count)])
    return value


def on_device(gate_acts, value_acts, kernel, norm_gain, out_grad):
    rows, width = value_acts.shape
    heads = kernel.shape[0]
    lag = kernel.shape[1] // 2
    count = lax.axis_size("seq")
    assert width == heads * HEAD and rows == lag and rows % TILE == 0
    assert count & (count - 1) == 0
    full_width = width * lax.axis_size("chan")
    gain = norm_gain.reshape(1, width)
    taps = kernel.astype(jnp.float32)

    size = rows // VALUE_CHUNKS
    ahead, behind = lax.optimization_barrier(
        (band_rows(taps[:, ::-1], 1, TILE - 1), band_rows(taps, 0, TILE))
    )
    band = bands(ahead)
    near, far = [], []
    for index in range(VALUE_CHUNKS):
        chunk = value_acts[index * size : (index + 1) * size]
        if index == 4:
            chunk = after(chunk, near[1])
        elif index > 4:
            chunk = after(chunk, far[index - 5])
        near.append(swapped(chunk))
        if index == 0:
            near[0], band = lax.optimization_barrier((near[0], band))
        far.append(relayed(near[index]))
    mixed, sums = forward(band, [value_acts], near, far, gate_acts, out_grad, gain, lag)
    sums = sum_over(sums, "chan")
    args = (sums, mixed, gate_acts, out_grad, gain)
    mix_grad = mix_grad_of(full_width, GRAD_CHUNKS, *args)

    grad_near = [swapped(chunk) for chunk in mix_grad]
    normed, gate_grad, gain_sums = norm(full_width, *args)
    pairs = heads // 2
    early = pairs // 2
    args = (gain_sums, [value_acts], near, far, mix_grad, lag)
    first = kernel_grad_local(0, early, *args)
    back_band = bands(after(behind, mix_grad[0]))
    grad_near[0], first, back_band = lax.optimization_barrier((grad_near[0], first, back_band))
    second = kernel_grad_local(early, pairs - early, *args)
    grad_near[1], first, second = lax.optimization_barrier((grad_near[1], first, second))
    grad_far = [relayed(chunk) for chunk in grad_near]
    totals = jnp.concatenate([first, second], axis=0)
    for bit in range(count.bit_length() - 1):
        if bit + 1 < GRAD_CHUNKS:
            totals, grad_far[bit] = lax.optimization_barrier((totals, grad_far[bit]))
        totals += lax.ppermute(totals, "seq", [(i, i ^ (1 << bit)) for i in range(count)])
    value_grad = value_grad_of(back_band, mix_grad, grad_near, grad_far, lag)
    tokens = rows * count
    kernel_grad = totals[:, : 2 * lag] / math.sqrt(tokens * HEAD)
    gain_grad = totals[:, 2 * lag : 2 * lag + HEAD].reshape(width) / math.sqrt(tokens)
    return (normed, gate_grad, value_grad, kernel_grad, gain_grad)


def solution(mesh):
    placed = (P("seq", "chan"), P("seq", "chan"), P("chan", None), P("chan"), P("seq", "chan"))
    return jax.shard_map(
        on_device,
        mesh=mesh,
        in_specs=placed,
        out_specs=(
            P("seq", "chan"),
            P("seq", "chan"),
            P("seq", "chan"),
            P("chan", None),
            P("chan"),
        ),
        check_vma=False,
    )
```

time: 206 us -> 171 us (0.83)
  local copies, waits for them, and re-layouts: 28 us -> 3.85 us
  starting transfers between devices: 54.9 us -> 71.9 us
  waiting for transfers between devices: 63.1 us -> 48.5 us
  Pallas kernels: 53.7 us -> 44.2 us
  blocking collectives: 2.45 us -> 0 us
    unnamed x29 -> x10, local copies, waits for them, and re-layouts: 20.4 us -> 0.03 us
    ppermute x20 -> x29, starting transfers between devices: 54.9 us -> 71.9 us  [the longest x12 46.4 us: relayed(): lax.ppermute(chunk, 'seq', [(i, j) for i, j in pairs if 0 <= j < count])]
    ppermute x20 -> x29, waiting for transfers between devices: 63.1 us -> 48.5 us  [the longest x12 22.2 us: swapped(): return lax.ppermute(chunk, 'seq', [(i, i ^ 1) for i in range(count)])]
    pallas_call x7 -> x8, Pallas kernels: 53.7 us -> 44.2 us  [the longest x2 11.7 us: kernel_grad_local(): pl.pallas_call(functools.partial(kernel_grad_body, first, slots, sizes),...]
    slice x2 -> x1, local copies, waits for them, and re-layouts: 4.73 us -> 1.71 us  [on_device(): chunk = value_acts[index * size:(index + 1) * size]]
    psum x1 -> x0, blocking collectives: 2.45 us -> none  [on_device(): sums = lax.psum(sums, 'chan')]
  transfers between devices with their start and end apart: 20 -> 29, of which waited for: 11 -> 16; matrix products, arithmetic and copies ran while one was open for 3% -> 1% of each run, Pallas kernels for 3% -> 19%
where the time goes in v2:
time: 171 us; the launch traced here: 170 us
  starting transfers between devices  71.9 us (42%)
  waiting for transfers between devices  48.5 us (28%)
  Pallas kernels  44.2 us (26%)
  local copies, waits for them, and re-layouts  3.85 us (2%)
    ppermute x12, starting transfers between devices, relayed(): lax.ppermute(chunk, 'seq', [(i, j) for i, j in pairs if 0 <= j < count])  46.4 us
    ppermute x12, waiting for transfers between devices, swapped(): return lax.ppermute(chunk, 'seq', [(i, i ^ 1) for i in range(count)])  22.2 us
    ppermute x4, waiting for transfers between devices, on_device(): lax.ppermute(totals, 'seq', [(i, i ^ 1 << bit) for i in range(count)])  18.3 us
    ppermute x12, starting transfers between devices, swapped(): return lax.ppermute(chunk, 'seq', [(i, i ^ 1) for i in range(count)])  15.7 us
    pallas_call x2, Pallas kernels, kernel_grad_local(): pl.pallas_call(functools.partial(kernel_grad_body, first, slots, sizes),...  11.7 us
    pallas_call x1, Pallas kernels, forward(): pl.pallas_call(functools.partial(forward_body, slots, sizes), grid=(width...  10.6 us
    pallas_call x1, Pallas kernels, value_grad_of(): pl.pallas_call(functools.partial(value_grad_body, slots, sizes), grid=(wi...  9.77 us
    ppermute x4, starting transfers between devices, on_device(): lax.ppermute(totals, 'seq', [(i, i ^ 1 << bit) for i in range(count)])  9.75 us
  transfers between devices with their start and end apart: 29, of which 16 were waited for; matrix products, arithmetic and copies ran while one was open for 1% of the time, Pallas kernels for 19%

profile of v2, /device:TPU:0, one launch (start us, length us, event | category | flops | bytes accessed | tf_op | source)
XLA Modules:
  0.0 170.3 jit_solution(13907396638176397619)
XLA Ops:
  12.5 4.0 %collective-permute-start.5 = (bf16[128,1024]{1,0:T(8,128)(2,1)S(1)}, bf16[128,1024]{1,0:T(8,128)(2,1)S(1)}, u32[]{:S(2)}, u32[]{:S(2)}) collective-permute-start(bf16[128,1024]{1,0:T(8,128)(2,1)S(1)} %collective-permute-done.refs_1_), channel_id=1, source_target_pairs={{0,4},{4,8},{6,2},{8,12},{10,6},{12,16},{14,10},{16,20},{18,14},{2... | collective-permute-start | bytes 786440 | tf_op jit(solution)/shard_map/ppermute | solution.py:418
  18.1 4.0 %collective-permute-start.7 = (bf16[128,1024]{1,0:T(8,128)(2,1)S(1)}, bf16[128,1024]{1,0:T(8,128)(2,1)S(1)}, u32[]{:S(2)}, u32[]{:S(2)}) collective-permute-start(bf16[128,1024]{1,0:T(8,128)(2,1)S(1)} %collective-permute-done.1.refs_2_), channel_id=1, source_target_pairs={{0,4},{4,8},{6,2},{8,12},{10,6},{12,16},{14,10},{16,20},{18,14},{2... | collective-permute-start | bytes 786440 | tf_op jit(solution)/shard_map/ppermute | solution.py:418
  22.9 3.7 %collective-permute-start.9 = (bf16[128,1024]{1,0:T(8,128)(2,1)S(1)}, bf16[128,1024]{1,0:T(8,128)(2,1)S(1)}, u32[]{:S(2)}, u32[]{:S(2)}) collective-permute-start(bf16[128,1024]{1,0:T(8,128)(2,1)S(1)} %collective-permute-done.2.refs_3_), channel_id=1, source_target_pairs={{0,4},{4,8},{6,2},{8,12},{10,6},{12,16},{14,10},{16,20},{18,14},{2... | collective-permute-start | bytes 786440 | tf_op jit(solution)/shard_map/ppermute | solution.py:418
  35.9 3.4 %collective-permute-start.11 = (bf16[128,1024]{1,0:T(8,128)(2,1)S(1)}, bf16[128,1024]{1,0:T(8,128)(2,1)S(1)}, u32[]{:S(2)}, u32[]{:S(2)}) collective-permute-start(bf16[128,1024]{1,0:T(8,128)(2,1)S(1)} %collective-permute-done.3.refs_4_), channel_id=1, source_target_pairs={{0,4},{4,8},{6,2},{8,12},{10,6},{12,16},{14,10},{16,20},{18,14},{2... | collective-permute-start | bytes 786440 | tf_op jit(solution)/shard_map/ppermute | solution.py:418
  41.5 3.4 %collective-permute-start.12 = (bf16[128,1024]{1,0:T(8,128)(2,1)S(1)}, bf16[128,1024]{1,0:T(8,128)(2,1)S(1)}, u32[]{:S(2)}, u32[]{:S(2)}) collective-permute-start(bf16[128,1024]{1,0:T(8,128)(2,1)S(1)} %collective-permute-done.4.refs_5_), channel_id=1, source_target_pairs={{0,4},{4,8},{6,2},{8,12},{10,6},{12,16},{14,10},{16,20},{18,14},{2... | collective-permute-start | bytes 786440 | tf_op jit(solution)/shard_map/ppermute | solution.py:418
  47.1 3.4 %collective-permute-start.13 = (bf16[128,1024]{1,0:T(8,128)(2,1)S(1)}, bf16[128,1024]{1,0:T(8,128)(2,1)S(1)}, u32[]{:S(2)}, u32[]{:S(2)}) collective-permute-start(bf16[128,1024]{1,0:T(8,128)(2,1)S(1)} %collective-permute-done.6.refs_6_), channel_id=1, source_target_pairs={{0,4},{4,8},{6,2},{8,12},{10,6},{12,16},{14,10},{16,20},{18,14},{2... | collective-permute-start | bytes 786440 | tf_op jit(solution)/shard_map/ppermute | solution.py:418
  52.7 3.4 %collective-permute-start.14 = (bf16[128,1024]{1,0:T(8,128)(2,1)S(1)}, bf16[128,1024]{1,0:T(8,128)(2,1)S(1)}, u32[]{:S(2)}, u32[]{:S(2)}) collective-permute-start(bf16[128,1024]{1,0:T(8,128)(2,1)S(1)} %collective-permute-done.8.refs_7_), channel_id=1, source_target_pairs={{0,4},{4,8},{6,2},{8,12},{10,6},{12,16},{14,10},{16,20},{18,14},{2... | collective-permute-start | bytes 786440 | tf_op jit(solution)/shard_map/ppermute | solution.py:418
  56.2 3.4 %collective-permute-start.15 = (bf16[128,1024]{1,0:T(8,128)(2,1)S(1)}, bf16[128,1024]{1,0:T(8,128)(2,1)S(1)}, u32[]{:S(2)}, u32[]{:S(2)}) collective-permute-start(bf16[128,1024]{1,0:T(8,128)(2,1)S(1)} %collective-permute-done.10.refs_8_), channel_id=1, source_target_pairs={{0,4},{4,8},{6,2},{8,12},{10,6},{12,16},{14,10},{16,20},{18,14},{2... | collective-permute-start | bytes 786440 | tf_op jit(solution)/shard_map/ppermute | solution.py:418
  59.6 3.1 %collective-permute-done.14.refs_15_ = bf16[128,1024]{1,0:T(8,128)(2,1)S(1)} collective-permute-done((bf16[128,1024]{1,0:T(8,128)(2,1)S(1)}, bf16[128,1024]{1,0:T(8,128)(2,1)S(1)}, u32[]{:S(2)}, u32[]{:S(2)}) %collective-permute-start.14) | collective-permute-done | bytes 262176 | tf_op jit(solution)/shard_map/ppermute | solution.py:418
  65.7 10.6 %forward.1 = (f32[1024,1024]{1,0:T(8,128)S(1)}, f32[2,1024]{1,0:T(2,128)S(1)}) custom-call(bf16[16,128,2432]{2,1,0:T(8,128)(2,1)S(1)} %bands.2.band_ref, bf16[1024,1024]{1,0:T(8,128)(2,1)S(1)} %copy-done.2, bf16[128,1024]{1,0:T(8,128)(2,1)S(1)} %collective-permute-done.refs_1_, bf16[128,1024]{1,0:T(8,128)(2,1)S(1)} %collective-permute-done.1.refs_2_, ...), custom_call_target="tpu_custom_call" | custom-call | flops 4831838208 | bytes 16777216 | tf_op jit(solution)/shard_map/forward/pallas_call | solution.py:203
  86.0 4.7 %norm.1 = (bf16[1024,1024]{1,0:T(8,128)(2,1)}, bf16[1024,1024]{1,0:T(8,128)(2,1)}, f32[1,1024]{1,0:T(1,128)S(1)}) custom-call(f32[2,1024]{1,0:T(2,128)S(1)} %add.19.sums_ref, f32[1024,1024]{1,0:T(8,128)S(1)} %get-tuple-element.43.mixed_ref, bf16[1024,1024]{1,0:T(8,128)(2,1)S(1)} %copy-done, bf16[1024,1024]{1,0:T(8,128)(2,1)S(1)} %copy-done.1, ...), custom_call_target="tpu_custom_call" | custom-call | flops 14680064 | bytes 12582912 | tf_op jit(solution)/shard_map/norm/pallas_call | solution.py:294
  90.7 5.8 %kernel_grad.2 = f32[8,2176]{1,0:T(8,128)S(1)} custom-call(f32[1,1024]{1,0:T(1,128)S(1)} %get-tuple-element.47.gain_ref, bf16[1024,1024]{1,0:T(8,128)(2,1)S(1)} %copy-done.2, bf16[128,1024]{1,0:T(8,128)(2,1)S(1)} %collective-permute-done.refs_1_, bf16[128,1024]{1,0:T(8,128)(2,1)S(1)} %collective-permute-done.1.refs_2_, ...), custom_call_target="tpu_custom_call" | custom-call | flops 2415919104 | bytes 4194304 | tf_op jit(solution)/shard_map/kernel_grad/pallas_call | solution.py:359
  96.5 4.4 %collective-permute-start.21 = (bf16[256,1024]{1,0:T(8,128)(2,1)S(1)}, bf16[256,1024]{1,0:T(8,128)(2,1)S(1)}, u32[]{:S(2)}, u32[]{:S(2)}) collective-permute-start(bf16[256,1024]{1,0:T(8,128)(2,1)S(1)} %collective-permute-done.17.refs_4_), channel_id=1, source_target_pairs={{0,4},{4,8},{6,2},{8,12},{10,6},{12,16},{14,10},{16,20},{18,14},{2... | collective-permute-start | bytes 1572872 | tf_op jit(solution)/shard_map/ppermute | solution.py:418
  101.0 5.9 %kernel_grad.3 = f32[8,2176]{1,0:T(8,128)S(1)} custom-call(f32[1,1024]{1,0:T(1,128)S(1)} %get-tuple-element.47.gain_ref, bf16[1024,1024]{1,0:T(8,128)(2,1)S(1)} %copy-done.2, bf16[128,1024]{1,0:T(8,128)(2,1)S(1)} %collective-permute-done.refs_1_, bf16[128,1024]{1,0:T(8,128)(2,1)S(1)} %collective-permute-done.1.refs_2_, ...), custom_call_target="tpu_custom_call" | custom-call | flops 2415919104 | bytes 4194304 | tf_op jit(solution)/shard_map/kernel_grad/pallas_call | solution.py:359
  106.9 4.3 %collective-permute-start.23 = (bf16[256,1024]{1,0:T(8,128)(2,1)S(1)}, bf16[256,1024]{1,0:T(8,128)(2,1)S(1)}, u32[]{:S(2)}, u32[]{:S(2)}) collective-permute-start(bf16[256,1024]{1,0:T(8,128)(2,1)S(1)} %collective-permute-done.18.refs_5_), channel_id=1, source_target_pairs={{0,4},{4,8},{6,2},{8,12},{10,6},{12,16},{14,10},{16,20},{18,14},{2... | collective-permute-start | bytes 1572872 | tf_op jit(solution)/shard_map/ppermute | solution.py:418
  111.2 4.8 %collective-permute-done.19.refs_6_ = bf16[256,1024]{1,0:T(8,128)(2,1)S(1)} collective-permute-done((bf16[256,1024]{1,0:T(8,128)(2,1)S(1)}, bf16[256,1024]{1,0:T(8,128)(2,1)S(1)}, u32[]{:S(2)}, u32[]{:S(2)}) %collective-permute-start.19) | collective-permute-done | bytes 524320 | tf_op jit(solution)/shard_map/ppermute | solution.py:412
  116.0 4.4 %collective-permute-start.25 = (bf16[256,1024]{1,0:T(8,128)(2,1)S(1)}, bf16[256,1024]{1,0:T(8,128)(2,1)S(1)}, u32[]{:S(2)}, u32[]{:S(2)}) collective-permute-start(bf16[256,1024]{1,0:T(8,128)(2,1)S(1)} %collective-permute-done.19.refs_6_), channel_id=1, source_target_pairs={{0,4},{4,8},{6,2},{8,12},{10,6},{12,16},{14,10},{16,20},{18,14},{2... | collective-permute-start | bytes 1572872 | tf_op jit(solution)/shard_map/ppermute | solution.py:418
  120.5 6.0 %collective-permute-done.20.refs_7_ = bf16[256,1024]{1,0:T(8,128)(2,1)S(1)} collective-permute-done((bf16[256,1024]{1,0:T(8,128)(2,1)S(1)}, bf16[256,1024]{1,0:T(8,128)(2,1)S(1)}, u32[]{:S(2)}, u32[]{:S(2)}) %collective-permute-start.20) | collective-permute-done | bytes 524320 | tf_op jit(solution)/shard_map/ppermute | solution.py:412
  126.5 4.4 %collective-permute-start.26 = (bf16[256,1024]{1,0:T(8,128)(2,1)S(1)}, bf16[256,1024]{1,0:T(8,128)(2,1)S(1)}, u32[]{:S(2)}, u32[]{:S(2)}) collective-permute-start(bf16[256,1024]{1,0:T(8,128)(2,1)S(1)} %collective-permute-done.20.refs_7_), channel_id=1, source_target_pairs={{0,4},{4,8},{6,2},{8,12},{10,6},{12,16},{14,10},{16,20},{18,14},{2... | collective-permute-start | bytes 1572872 | tf_op jit(solution)/shard_map/ppermute | solution.py:418
  131.0 5.0 %collective-permute-done.22 = f32[16,2176]{1,0:T(8,128)S(1)} collective-permute-done((f32[16,2176]{1,0:T(8,128)S(1)}, f32[16,2176]{1,0:T(8,128)S(1)}, u32[]{:S(2)}, u32[]{:S(2)}) %collective-permute-start.22) | collective-permute-done | bytes 139296 | tf_op jit(solution)/shard_map/ppermute | solution.py:477
  138.6 9.4 %collective-permute-done.24 = f32[16,2176]{1,0:T(8,128)S(1)} collective-permute-done((f32[16,2176]{1,0:T(8,128)S(1)}, f32[16,2176]{1,0:T(8,128)S(1)}, u32[]{:S(2)}, u32[]{:S(2)}) %collective-permute-start.24) | collective-permute-done | bytes 139296 | tf_op jit(solution)/shard_map/ppermute | solution.py:477
  148.0 4.4 %collective-permute-start.27 = (f32[16,2176]{1,0:T(8,128)S(1)}, f32[16,2176]{1,0:T(8,128)S(1)}, u32[]{:S(2)}, u32[]{:S(2)}) collective-permute-start(f32[16,2176]{1,0:T(8,128)S(1)} %add.21), channel_id=1, source_target_pairs={{0,8},{2,10},{4,12},{6,14},{8,0},{10,2},{12,4},{14,6},{16,24},{18,... | collective-permute-start | bytes 417800 | tf_op jit(solution)/shard_map/ppermute | solution.py:477
  152.4 3.9 %collective-permute-done.27 = f32[16,2176]{1,0:T(8,128)S(1)} collective-permute-done((f32[16,2176]{1,0:T(8,128)S(1)}, f32[16,2176]{1,0:T(8,128)S(1)}, u32[]{:S(2)}, u32[]{:S(2)}) %collective-permute-start.27) | collective-permute-done | bytes 139296 | tf_op jit(solution)/shard_map/ppermute | solution.py:477
  159.1 9.8 %value_grad.1 = bf16[1024,1024]{1,0:T(8,128)(2,1)} custom-call(bf16[16,128,2432]{2,1,0:T(8,128)(2,1)S(1)} %bands.3.band_ref, bf16[256,1024]{1,0:T(8,128)(2,1)S(1)} %get-tuple-element.46.refs_17_.refs_0_, bf16[256,1024]{1,0:T(8,128)(2,1)S(1)} %get-tuple-element.48.refs_18_.refs_1_, bf16[256,1024]{1,0:T(8,128)(2,1)S(1)} %get-tuple-element.49.refs_19_.refs_2_, ...), custom_call_target="tpu_custom_call" | custom-call | flops 4831838208 | bytes 12582912 | tf_op jit(solution)/shard_map/value_grad/pallas_call | solution.py:397
  (67 shorter events, 49.5 us)
Async XLA Ops:
  2.4 10.1 %collective-permute-start = (bf16[128,1024]{1,0:T(8,128)(2,1)S(1)}, bf16[128,1024]{1,0:T(8,128)(2,1)S(1)}, u32[]{:S(2)}, u32[]{:S(2)}) collective-permute-start(bf16[128,1024]{1,0:T(8,128)(2,1)S(1)} %get-tuple-element.72), channel_id=1, source_target_pairs={{0,2},{2,0},{4,6},{6,4},{8,10},{10,8},{12,14},{14,12},{16,18},{18,... | collective-permute-start | bytes 786440 | tf_op jit(solution)/shard_map/ppermute | solution.py:412
  5.4 12.8 %collective-permute-start.1 = (bf16[128,1024]{1,0:T(8,128)(2,1)S(1)}, bf16[128,1024]{1,0:T(8,128)(2,1)S(1)}, u32[]{:S(2)}, u32[]{:S(2)}) collective-permute-start(bf16[128,1024]{1,0:T(8,128)(2,1)S(1)} %get-tuple-element.71), channel_id=1, source_target_pairs={{0,2},{2,0},{4,6},{6,4},{8,10},{10,8},{12,14},{14,12},{16,18},{18,... | collective-permute-start | bytes 786440 | tf_op jit(solution)/shard_map/ppermute | solution.py:412
  5.4 17.5 %collective-permute-start.2 = (bf16[128,1024]{1,0:T(8,128)(2,1)S(1)}, bf16[128,1024]{1,0:T(8,128)(2,1)S(1)}, u32[]{:S(2)}, u32[]{:S(2)}) collective-permute-start(bf16[128,1024]{1,0:T(8,128)(2,1)S(1)} %get-tuple-element.70), channel_id=1, source_target_pairs={{0,2},{2,0},{4,6},{6,4},{8,10},{10,8},{12,14},{14,12},{16,18},{18,... | collective-permute-start | bytes 786440 | tf_op jit(solution)/shard_map/ppermute | solution.py:412
  12.5 16.2 %collective-permute-start.5 = (bf16[128,1024]{1,0:T(8,128)(2,1)S(1)}, bf16[128,1024]{1,0:T(8,128)(2,1)S(1)}, u32[]{:S(2)}, u32[]{:S(2)}) collective-permute-start(bf16[128,1024]{1,0:T(8,128)(2,1)S(1)} %collective-permute-done.refs_1_), channel_id=1, source_target_pairs={{0,4},{4,8},{6,2},{8,12},{10,6},{12,16},{14,10},{16,20},{18,14},{2... | collective-permute-start | bytes 786440 | tf_op jit(solution)/shard_map/ppermute | solution.py:418
  18.1 10.7 %collective-permute-start.7 = (bf16[128,1024]{1,0:T(8,128)(2,1)S(1)}, bf16[128,1024]{1,0:T(8,128)(2,1)S(1)}, u32[]{:S(2)}, u32[]{:S(2)}) collective-permute-start(bf16[128,1024]{1,0:T(8,128)(2,1)S(1)} %collective-permute-done.1.refs_2_), channel_id=1, source_target_pairs={{0,4},{4,8},{6,2},{8,12},{10,6},{12,16},{14,10},{16,20},{18,14},{2... | collective-permute-start | bytes 786440 | tf_op jit(solution)/shard_map/ppermute | solution.py:418
  26.7 14.8 %collective-permute-start.4 = (bf16[128,1024]{1,0:T(8,128)(2,1)S(1)}, bf16[128,1024]{1,0:T(8,128)(2,1)S(1)}, u32[]{:S(2)}, u32[]{:S(2)}) collective-permute-start(bf16[128,1024]{1,0:T(8,128)(2,1)S(1)} %get-tuple-element.38), channel_id=1, source_target_pairs={{0,2},{2,0},{4,6},{6,4},{8,10},{10,8},{12,14},{14,12},{16,18},{18,... | collective-permute-start | bytes 786440 | tf_op jit(solution)/shard_map/ppermute | solution.py:412
  28.7 18.4 %collective-permute-start.6 = (bf16[128,1024]{1,0:T(8,128)(2,1)S(1)}, bf16[128,1024]{1,0:T(8,128)(2,1)S(1)}, u32[]{:S(2)}, u32[]{:S(2)}) collective-permute-start(bf16[128,1024]{1,0:T(8,128)(2,1)S(1)} %get-tuple-element.39), channel_id=1, source_target_pairs={{0,2},{2,0},{4,6},{6,4},{8,10},{10,8},{12,14},{14,12},{16,18},{18,... | collective-permute-start | bytes 786440 | tf_op jit(solution)/shard_map/ppermute | solution.py:412
  28.8 24.0 %collective-permute-start.8 = (bf16[128,1024]{1,0:T(8,128)(2,1)S(1)}, bf16[128,1024]{1,0:T(8,128)(2,1)S(1)}, u32[]{:S(2)}, u32[]{:S(2)}) collective-permute-start(bf16[128,1024]{1,0:T(8,128)(2,1)S(1)} %get-tuple-element.40), channel_id=1, source_target_pairs={{0,2},{2,0},{4,6},{6,4},{8,10},{10,8},{12,14},{14,12},{16,18},{18,... | collective-permute-start | bytes 786440 | tf_op jit(solution)/shard_map/ppermute | solution.py:412
  31.6 24.6 %collective-permute-start.10 = (bf16[128,1024]{1,0:T(8,128)(2,1)S(1)}, bf16[128,1024]{1,0:T(8,128)(2,1)S(1)}, u32[]{:S(2)}, u32[]{:S(2)}) collective-permute-start(bf16[128,1024]{1,0:T(8,128)(2,1)S(1)} %get-tuple-element.41), channel_id=1, source_target_pairs={{0,2},{2,0},{4,6},{6,4},{8,10},{10,8},{12,14},{14,12},{16,18},{18,... | collective-permute-start | bytes 786440 | tf_op jit(solution)/shard_map/ppermute | solution.py:412
  35.9 23.7 %collective-permute-start.11 = (bf16[128,1024]{1,0:T(8,128)(2,1)S(1)}, bf16[128,1024]{1,0:T(8,128)(2,1)S(1)}, u32[]{:S(2)}, u32[]{:S(2)}) collective-permute-start(bf16[128,1024]{1,0:T(8,128)(2,1)S(1)} %collective-permute-done.3.refs_4_), channel_id=1, source_target_pairs={{0,4},{4,8},{6,2},{8,12},{10,6},{12,16},{14,10},{16,20},{18,14},{2... | collective-permute-start | bytes 786440 | tf_op jit(solution)/shard_map/ppermute | solution.py:418
  41.5 18.1 %collective-permute-start.12 = (bf16[128,1024]{1,0:T(8,128)(2,1)S(1)}, bf16[128,1024]{1,0:T(8,128)(2,1)S(1)}, u32[]{:S(2)}, u32[]{:S(2)}) collective-permute-start(bf16[128,1024]{1,0:T(8,128)(2,1)S(1)} %collective-permute-done.4.refs_5_), channel_id=1, source_target_pairs={{0,4},{4,8},{6,2},{8,12},{10,6},{12,16},{14,10},{16,20},{18,14},{2... | collective-permute-start | bytes 786440 | tf_op jit(solution)/shard_map/ppermute | solution.py:418
  47.1 12.5 %collective-permute-start.13 = (bf16[128,1024]{1,0:T(8,128)(2,1)S(1)}, bf16[128,1024]{1,0:T(8,128)(2,1)S(1)}, u32[]{:S(2)}, u32[]{:S(2)}) collective-permute-start(bf16[128,1024]{1,0:T(8,128)(2,1)S(1)} %collective-permute-done.6.refs_6_), channel_id=1, source_target_pairs={{0,4},{4,8},{6,2},{8,12},{10,6},{12,16},{14,10},{16,20},{18,14},{2... | collective-permute-start | bytes 786440 | tf_op jit(solution)/shard_map/ppermute | solution.py:418
  52.7 10.0 %collective-permute-start.14 = (bf16[128,1024]{1,0:T(8,128)(2,1)S(1)}, bf16[128,1024]{1,0:T(8,128)(2,1)S(1)}, u32[]{:S(2)}, u32[]{:S(2)}) collective-permute-start(bf16[128,1024]{1,0:T(8,128)(2,1)S(1)} %collective-permute-done.8.refs_7_), channel_id=1, source_target_pairs={{0,4},{4,8},{6,2},{8,12},{10,6},{12,16},{14,10},{16,20},{18,14},{2... | collective-permute-start | bytes 786440 | tf_op jit(solution)/shard_map/ppermute | solution.py:418
  56.2 9.5 %collective-permute-start.15 = (bf16[128,1024]{1,0:T(8,128)(2,1)S(1)}, bf16[128,1024]{1,0:T(8,128)(2,1)S(1)}, u32[]{:S(2)}, u32[]{:S(2)}) collective-permute-start(bf16[128,1024]{1,0:T(8,128)(2,1)S(1)} %collective-permute-done.10.refs_8_), channel_id=1, source_target_pairs={{0,4},{4,8},{6,2},{8,12},{10,6},{12,16},{14,10},{16,20},{18,14},{2... | collective-permute-start | bytes 786440 | tf_op jit(solution)/shard_map/ppermute | solution.py:418
  78.7 17.8 %collective-permute-start.17 = (bf16[256,1024]{1,0:T(8,128)(2,1)S(1)}, bf16[256,1024]{1,0:T(8,128)(2,1)S(1)}, u32[]{:S(2)}, u32[]{:S(2)}) collective-permute-start(bf16[256,1024]{1,0:T(8,128)(2,1)S(1)} %get-tuple-element.46.refs_17_.refs_0_), channel_id=1, source_target_pairs={{0,2},{2,0},{4,6},{6,4},{8,10},{10,8},{12,14},{14,12},{16,18},{18,... | collective-permute-start | bytes 1572872 | tf_op jit(solution)/shard_map/ppermute | solution.py:412
  79.8 27.1 %collective-permute-start.18 = (bf16[256,1024]{1,0:T(8,128)(2,1)S(1)}, bf16[256,1024]{1,0:T(8,128)(2,1)S(1)}, u32[]{:S(2)}, u32[]{:S(2)}) collective-permute-start(bf16[256,1024]{1,0:T(8,128)(2,1)S(1)} %get-tuple-element.48.refs_18_.refs_1_), channel_id=1, source_target_pairs={{0,2},{2,0},{4,6},{6,4},{8,10},{10,8},{12,14},{14,12},{16,18},{18,... | collective-permute-start | bytes 1572872 | tf_op jit(solution)/shard_map/ppermute | solution.py:412
  80.8 35.2 %collective-permute-start.19 = (bf16[256,1024]{1,0:T(8,128)(2,1)S(1)}, bf16[256,1024]{1,0:T(8,128)(2,1)S(1)}, u32[]{:S(2)}, u32[]{:S(2)}) collective-permute-start(bf16[256,1024]{1,0:T(8,128)(2,1)S(1)} %get-tuple-element.49.refs_19_.refs_2_), channel_id=1, source_target_pairs={{0,2},{2,0},{4,6},{6,4},{8,10},{10,8},{12,14},{14,12},{16,18},{18,... | collective-permute-start | bytes 1572872 | tf_op jit(solution)/shard_map/ppermute | solution.py:412
  81.8 44.7 %collective-permute-start.20 = (bf16[256,1024]{1,0:T(8,128)(2,1)S(1)}, bf16[256,1024]{1,0:T(8,128)(2,1)S(1)}, u32[]{:S(2)}, u32[]{:S(2)}) collective-permute-start(bf16[256,1024]{1,0:T(8,128)(2,1)S(1)} %get-tuple-element.50.refs_20_.refs_3_), channel_id=1, source_target_pairs={{0,2},{2,0},{4,6},{6,4},{8,10},{10,8},{12,14},{14,12},{16,18},{18,... | collective-permute-start | bytes 1572872 | tf_op jit(solution)/shard_map/ppermute | solution.py:412
  96.5 34.4 %collective-permute-start.21 = (bf16[256,1024]{1,0:T(8,128)(2,1)S(1)}, bf16[256,1024]{1,0:T(8,128)(2,1)S(1)}, u32[]{:S(2)}, u32[]{:S(2)}) collective-permute-start(bf16[256,1024]{1,0:T(8,128)(2,1)S(1)} %collective-permute-done.17.refs_4_), channel_id=1, source_target_pairs={{0,4},{4,8},{6,2},{8,12},{10,6},{12,16},{14,10},{16,20},{18,14},{2... | collective-permute-start | bytes 1572872 | tf_op jit(solution)/shard_map/ppermute | solution.py:418
  106.9 29.2 %collective-permute-start.23 = (bf16[256,1024]{1,0:T(8,128)(2,1)S(1)}, bf16[256,1024]{1,0:T(8,128)(2,1)S(1)}, u32[]{:S(2)}, u32[]{:S(2)}) collective-permute-start(bf16[256,1024]{1,0:T(8,128)(2,1)S(1)} %collective-permute-done.18.refs_5_), channel_id=1, source_target_pairs={{0,4},{4,8},{6,2},{8,12},{10,6},{12,16},{14,10},{16,20},{18,14},{2... | collective-permute-start | bytes 1572872 | tf_op jit(solution)/shard_map/ppermute | solution.py:418
  116.0 32.0 %collective-permute-start.25 = (bf16[256,1024]{1,0:T(8,128)(2,1)S(1)}, bf16[256,1024]{1,0:T(8,128)(2,1)S(1)}, u32[]{:S(2)}, u32[]{:S(2)}) collective-permute-start(bf16[256,1024]{1,0:T(8,128)(2,1)S(1)} %collective-permute-done.19.refs_6_), channel_id=1, source_target_pairs={{0,4},{4,8},{6,2},{8,12},{10,6},{12,16},{14,10},{16,20},{18,14},{2... | collective-permute-start | bytes 1572872 | tf_op jit(solution)/shard_map/ppermute | solution.py:418
  126.5 32.6 %collective-permute-start.26 = (bf16[256,1024]{1,0:T(8,128)(2,1)S(1)}, bf16[256,1024]{1,0:T(8,128)(2,1)S(1)}, u32[]{:S(2)}, u32[]{:S(2)}) collective-permute-start(bf16[256,1024]{1,0:T(8,128)(2,1)S(1)} %collective-permute-done.20.refs_7_), channel_id=1, source_target_pairs={{0,4},{4,8},{6,2},{8,12},{10,6},{12,16},{14,10},{16,20},{18,14},{2... | collective-permute-start | bytes 1572872 | tf_op jit(solution)/shard_map/ppermute | solution.py:418
  136.1 11.9 %collective-permute-start.24 = (f32[16,2176]{1,0:T(8,128)S(1)}, f32[16,2176]{1,0:T(8,128)S(1)}, u32[]{:S(2)}, u32[]{:S(2)}) collective-permute-start(f32[16,2176]{1,0:T(8,128)S(1)} %add.20), channel_id=1, source_target_pairs={{0,4},{2,6},{4,0},{6,2},{8,12},{10,14},{12,8},{14,10},{16,20},{18,... | collective-permute-start | bytes 417800 | tf_op jit(solution)/shard_map/ppermute | solution.py:477
  156.3 12.6 %collective-permute-start.28 = (f32[16,2176]{1,0:T(8,128)S(1)}, f32[16,2176]{1,0:T(8,128)S(1)}, u32[]{:S(2)}, u32[]{:S(2)}) collective-permute-start(f32[16,2176]{1,0:T(8,128)S(1)} %add.22), channel_id=1, source_target_pairs={{0,16},{2,18},{4,20},{6,22},{8,24},{10,26},{12,28},{14,30},{16,0},... | collective-permute-start | bytes 417800 | tf_op jit(solution)/shard_map/ppermute | solution.py:477
  (10 other events, 266.4 us)
